TPU v7x, 32 devices: a whole 2x2x4 slice. The times are simulated.
32 devices in a mesh: row: 4 (over x, core), grid: 8 (over z, y).
Axes of the slice: x: 2, y: 2, z: 4, core: 2. Of those that a mesh axis runs over, the one named last changes fastest.
Arguments:
- cholesky: float32 [8, 153600], P('row'), may hold values from -6 to 6
- factor: float32 [1200, 6144], P('row', 'grid'), may hold values from -6 to 6
- core: float32 [6144, 128], P('grid'), may hold values from -0.078125 to 0.078125
Outputs:
- residual: float32 [8, 153600], P('row')
- core_grad: float32 [6144, 128], P('grid')
- factor_grad: float32 [1200, 6144], P('row', 'grid')
All inputs are finite; a program needn't handle non-finite values.
Results may differ from a plain program's by a relative error of at most 0.00012.
Values sent between devices are 32-bit elements; how exact they have to be, the bound alone decides.
A program may use at most 64 MiB of HBM per device.

v0:
```python
import jax
import jax.numpy as jnp
from jax import lax
from jax.sharding import PartitionSpec as P

N = 1200
G = 6144
K = 128


def per_device(cholesky, factor, core):
    hi = lax.Precision.HIGHEST
    count = cholesky.shape[0]
    vectors = core.shape[1]
    orbitals = lax.all_gather(factor, "row", axis=0, tiled=True)
    total_orb = orbitals.shape[0]
    slab = cholesky.reshape(count, total_orb, vectors)
    offset = lax.axis_index("row") * count
    first = lax.dynamic_slice_in_dim(orbitals, offset, count, 0)
    pair = first[:, None, :] * orbitals[None, :, :]
    partial_fit = jnp.einsum("pqg,gk->pqk", pair, core, precision=hi)
    fitted = lax.psum(partial_fit, "grid")
    whole_res = slab - fitted
    pairs_all = count * lax.axis_size("row") * total_orb
    core_part = jnp.einsum("pqg,pqk->gk", pair, whole_res, precision=hi)
    core_grad = -(1.0 / jnp.sqrt(jnp.float32(pairs_all))) * lax.psum(core_part, "row")
    proj = jnp.einsum("pqk,gk->pqg", whole_res, core, precision=hi)
    outer = jnp.einsum("pqg,pg->qg", proj, first, precision=hi)
    inner = jnp.einsum("pqg,qg->pg", proj, orbitals, precision=hi)
    current = lax.dynamic_slice_in_dim(outer, offset, count, 0)
    total = lax.dynamic_update_slice_in_dim(outer, current + inner, offset, 0)
    summed = lax.psum_scatter(total, "row", scatter_dimension=0, tiled=True)
    factor_grad = -jnp.sqrt(jnp.float32(G) / jnp.float32(N * K)) * summed
    return (whole_res.reshape(count, total_orb * vectors), core_grad, factor_grad)


def solution(mesh):
    placed = (P("row", None), P("row", "grid"), P("grid", None))
    return jax.shard_map(
        per_device,
        mesh=mesh,
        in_specs=placed,
        out_specs=(P("row", None), P("grid", None), P("row", "grid")),
        check_vma=False,
    )
```

profile of v0, /device:TPU:0, one launch (start us, length us, event | category | flops | bytes accessed | tf_op | source)
XLA Modules:
  0.0 247.4 jit_solution(16748297244567003438)
XLA Ops:
  7.2 0.0 copy-start
  7.2 0.0 all-gather.3.cloned.1.call-start
  7.2 0.7 all-gather.3.cloned.1.call-update
  7.9 0.0 all-reduce.5.cloned.1.call-start
  8.0 36.2 %all-gather.3.cloned.1.call-done = f32[4,300,768]{2,1,0:T(8,128)} async-done(((f32[1,300,768]{2,1,0:T(8,128)}), f32[4,300,768]{2,1,0:T(8,128)}) %all-gather.3.cloned.1.call-update) | async-done | bytes 3686416 | tf_op jit(solution)/shard_map/all_gather | solution.py:15
  44.2 3.5 %reshape.17 = f32[1200,768]{1,0:T(8,128)} reshape(f32[4,300,768]{2,1,0:T(8,128)} %all-gather.3.cloned.1.call-done) | data formatting | bytes 7372800
  47.7 0.8 constant_dynamic-slice_fusion
  48.5 9.1 %fusion.3 = f32[2,1200,128]{2,1,0:T(8,128)} fusion(f32[1200,768]{1,0:T(8,128)} %reshape.17, f32[2,768]{1,0:T(2,128)S(1)} %constant_dynamic-slice_fusion, f32[768,128]{1,0:T(8,128)S(1)} %copy-done), kind=kOutput, calls=%fused_computation.2 | convolution fusion | flops 2832998400 | bytes 5314560 | tf_op jit(solution)/shard_map/pqg,gk->pqk/dot_general | solution.py:21
  57.6 0.0 all-reduce.5.cloned.1.call-update
  57.6 0.2 all-reduce.7.cloned.1.call-start
  57.8 0.0 copy-done.4
  57.9 0.6 dynamic-slice.5
  59.1 0.8 fusion.16
  59.8 79.0 %all-reduce.5.cloned.1.call-done = f32[2,1200,128]{2,1,0:T(8,128)} async-done(((f32[2,1200,128]{2,1,0:T(8,128)}), f32[2,1200,128]{2,1,0:T(8,128)}) %all-reduce.5.cloned.1.call-update) | async-done | bytes 1228816 | tf_op jit(solution)/shard_map/psum | solution.py:22
  138.9 8.3 %multiply_reduce_fusion.1 = (f32[768,1200]{0,1:T(8,128)S(1)}, f32[2,1200,768]{2,1,0:T(8,128)S(1)}) fusion(f32[768,2]{0,1:T(2,128)S(1)} %fusion.16, f32[768,128]{1,0:T(8,128)S(1)} %copy-done, f32[2,1200,128]{2,1,0:T(8,128)} %all-reduce.5.cloned.1.call-done, f32[1,2,1200,128]{3,1,2,0:T(2,128)S(1)} %bitcast.39), kind=kOutput, calls=%fused_computation.5 | convolution fusion | flops 2834227200 | bytes 13916160 | tf_op jit(solution)/shard_map/pqk,gk->pqg/dot_general | solution.py:27
  147.2 0.0 copy-start.1
  147.2 1.9 copy.33
  149.1 1.5 copy-done.1
  150.6 1.3 multiply_reduce_fusion
  151.9 0.6 bitcast_dynamic-update-slice_fusion
  152.5 37.6 %fusion = f32[304,768]{1,0:T(8,128)} fusion(f32[1200,768]{1,0:T(8,128)} %bitcast_dynamic-update-slice_fusion), kind=kCustom, calls=%all-reduce-scatter | all-reduce-scatter fusion | flops 933889 | bytes 4620800
  190.2 0.8 slice
  191.0 1.5 collective-permute-start
  192.5 14.6 %fusion.9 = f32[768,128]{1,0:T(8,128)} fusion(f32[1200,768]{1,0:T(8,128)} %reshape.17, f32[2,768]{1,0:T(2,128)S(1)} %constant_dynamic-slice_fusion, f32[2,1200,128]{2,1,0:T(8,128)S(1)} %copy-done.3, f32[1,2,1200,128]{3,1,2,0:T(2,128)S(1)} %bitcast.40), kind=kOutput, calls=%fused_computation.12 | convolution fusion | flops 2833305600 | bytes 6543360 | tf_op jit(solution)/shard_map/pqg,pqk->gk/dot_general | solution.py:25
  207.1 0.0 all-reduce.7.cloned.1.call-update
  207.1 0.1 fusion.15
  207.2 4.7 %copy.30 = f32[1,2,1200,128]{3,1,2,0:T(2,128)} copy(f32[1,2,1200,128]{3,2,1,0:T(8,128)S(1)} %fusion.15) | data formatting | bytes 2457600
  211.9 0.0 collective-permute-done
  211.9 2.3 concatenate
  214.2 1.0 dynamic-slice_multiply_fusion
  215.2 23.9 %all-reduce.7.cloned.1.call-done = f32[768,128]{1,0:T(8,128)} async-done(((f32[768,128]{1,0:T(8,128)}), f32[768,128]{1,0:T(8,128)}) %all-reduce.7.cloned.1.call-update) | async-done | bytes 393232 | tf_op jit(solution)/shard_map/psum | solution.py:26
  239.1 1.8 broadcast_multiply_fusion
  (6 shorter events, 0.0 us)
Async XLA Ops:
  7.2 41.4 %copy-start = (f32[768,128]{1,0:T(8,128)S(1)}, f32[768,128]{1,0:T(8,128)}, u32[]{:S(2)}) copy-start(f32[768,128]{1,0:T(8,128)} %param.5) | copy-start | bytes 1179652
  7.2 37.0 %all-gather.3.cloned.1.call-start = ((), (), s32[]{:S(2)}) async-start(), calls=%async_computation.2 | async-start | bytes 4669440 | tf_op jit(solution)/shard_map/all_gather | solution.py:15
  7.9 131.0 %all-reduce.5.cloned.1.call-start = ((), (), s32[]{:S(2)}) async-start(), calls=%async_computation | async-start | bytes 2457600 | tf_op jit(solution)/shard_map/psum | solution.py:22
  47.7 10.2 %copy-start.4 = (u32[32]{0:T(128)S(1)}, u32[32]{0:T(128)}, u32[]{:S(2)}) copy-start(u32[32]{0:T(128)} %constant.20) | copy-start | bytes 388
  47.7 91.2 %copy-start.2 = (f32[2,153600]{1,0:T(2,128)S(1)}, f32[2,153600]{1,0:T(2,128)}, u32[]{:S(2)}) copy-start(f32[2,153600]{1,0:T(2,128)} %param.3) | copy-start | bytes 3686404
  57.6 181.5 %all-reduce.7.cloned.1.call-start = ((), (), s32[]{:S(2)}) async-start(), calls=%async_computation.1 | async-start | bytes 786432 | tf_op jit(solution)/shard_map/psum | solution.py:26
  147.2 3.4 %copy-start.1 = (f32[1200,768]{1,0:T(8,128)S(1)}, f32[1200,768]{1,0:T(8,128)}, u32[]{:S(2)}) copy-start(f32[1200,768]{1,0:T(8,128)} %reshape.17) | copy-start | bytes 11059204
  151.9 40.6 %copy-start.3 = (f32[2,1200,128]{2,1,0:T(8,128)S(1)}, f32[2,1200,128]{2,1,0:T(8,128)}, u32[]{:S(2)}) copy-start(f32[2,1200,128]{2,1,0:T(8,128)} %all-reduce.5.cloned.1.call-done) | copy-start | bytes 3686404
  191.0 20.9 %collective-permute-start = (f32[12,768]{1,0:T(8,128)S(1)}, f32[12,768]{1,0:T(8,128)S(1)}, u32[]{:S(2)}, u32[]{:S(2)}) collective-permute-start(f32[12,768]{1,0:T(8,128)S(1)} %slice), channel_id=1, source_target_pairs={{0,8},{8,16},{16,24},{1,9},{9,17},{17,25},{2,10},{10,18},{18,26},{... | collective-permute-start | bytes 110600
Sparse Core Ops, SparseCore 0:
  9.6 34.5 all-gather.2
  57.7 81.1 all-reduce.4
  207.2 31.8 all-reduce.6
where the time goes:
time: 248 us; the launch traced here: 247 us
  waiting for transfers between devices  140 us (56%)
  blocking collectives  37.6 us (15%)
  matrix products  32 us (13%)
  local copies, waits for them, and re-layouts  16.8 us (7%)
  between operations  14.5 us (6%)
  other arithmetic  4.87 us (2%)
    psum x1, waiting for transfers between devices, per_device(): fitted = lax.psum(partial_fit, 'grid')  79 us
    unnamed x1, blocking collectives  37.6 us
    all_gather x1, waiting for transfers between devices, per_device(): orbitals = lax.all_gather(factor, 'row', axis=0, tiled=True)  36.2 us
    psum x1, waiting for transfers between devices, per_device(): lax.psum(core_part, 'row')  23.9 us
    unnamed x17, local copies, waits for them, and re-layouts  16 us
    dot_general x1, matrix products, per_device(): core_part = jnp.einsum('pqg,pqk->gk', pair, whole_res, precision=hi)  14.6 us
    dot_general x1, matrix products, per_device(): partial_fit = jnp.einsum('pqg,gk->pqk', pair, core, precision=hi)  9.07 us
    dot_general x1, matrix products, per_device(): proj = jnp.einsum('pqk,gk->pqg', whole_res, core, precision=hi)  8.32 us
  transfers between devices with their start and end apart: 4, of which 3 were waited for; matrix products, arithmetic and copies ran while one was open for 10% of the time, Pallas kernels for 0%

commit v1 on v0

v1 whole, which is shorter than its diff:
```python
import functools
import math

import jax
import jax.numpy as jnp
from jax import lax
from jax.experimental import pallas as pl
from jax.experimental.pallas import tpu as pltpu
from jax.sharding import PartitionSpec as P

MESH = pl.DeviceIdType.MESH
F32 = jnp.float32
BF16 = jnp.bfloat16


def two_factors(n):
    fast = max(d for d in range(1, n + 1) if n % d == 0 and d * d <= n)
    return n // fast, fast


def split(x):
    hi = x.astype(BF16)
    return hi, (x - hi.astype(F32)).astype(BF16)


def dot3(left, right, dims):
    one = functools.partial(lax.dot_general, dimension_numbers=(dims, ((), ())), preferred_element_type=F32)
    return one(left[0], right[0]) + (one(left[0], right[1]) + one(left[1], right[0]))


def kernel(cfg, x_ref, core_ref, chol_ref, res_ref, cg_ref, fg_ref,
           xpad, xhi, xlo, x8, x8b, vhi, vlo, fit, rec_y, sum_y, rec_z, cbuf, resid, outer, cg, cols,
           cg_core, cg_half, cg_row, cg_fin, inner, inner_rec,
           x8_s, x8_r, c_s, c_r, y_s, y_r, z_s, z_r, gz_s, gz_r, gy_s, gy_r, p_s, p_r, i_s, i_r, k_s, k_r, h_s, h_r, f_s, f_r):
    nrow, slow, fast, npp, rows, rpad, vec, cg_scale, fg_scale = cfg
    ngrid = slow * fast
    np_all = npp * ngrid
    per_row = ngrid // nrow
    pts = x_ref.shape[1]
    half = pts // 2
    r = lax.axis_index("row")
    j = lax.axis_index("grid")
    a = j // fast
    b = j % fast
    owner = j // per_row

    def remote(src, dst, ssem, rsem, **device):
        return pltpu.make_async_remote_copy(src_ref=src, dst_ref=dst, send_sem=ssem, recv_sem=rsem, device_id=device, device_id_type=MESH)

    barrier = pltpu.get_barrier_semaphore()
    for e in range(1, nrow):
        pl.semaphore_signal(barrier, inc=1, device_id={"row": (r + e) % nrow}, device_id_type=MESH)
    for e in range(1, ngrid):
        pl.semaphore_signal(barrier, inc=1, device_id={"grid": (j + e) % ngrid}, device_id_type=MESH)
    pl.semaphore_wait(barrier, nrow + ngrid - 2)

    def x8_copy(e):
        return remote(x8, x8, x8_s.at[e - 1], x8_r.at[0], row=(r + e) % nrow)

    def c_copy(e):
        to = (r + e) % nrow
        return remote(chol_ref.at[to], cbuf, c_s.at[e - 1], c_r.at[0], row=to)

    @pl.when(r == 0)
    def _():
        x8[...] = x_ref[0:np_all, :]
        for e in range(1, nrow):
            x8_copy(e).start()

    @pl.when(r == owner)
    def _():
        for e in range(1, nrow):
            c_copy(e).start()
        cbuf[...] = chol_ref[r]

    xpad[rpad - 16:rpad, :] = jnp.zeros((16, pts), F32)
    xpad[0:rows, :] = x_ref[...]
    hi, lo = split(xpad[...])
    xhi[...] = hi
    xlo[...] = lo

    @pl.when(r != 0)
    def _():
        x8_copy(1).wait_recv()

    flip = jnp.transpose(jnp.concatenate([x8[...], jnp.zeros((vec - np_all, pts), F32)], axis=0))
    for p in range(np_all):
        x8b[p] = jnp.broadcast_to(flip[:, p:p + 1], (pts, vec))

    def y_copy(d, e):
        to = (b + e) % fast
        group = (a + d) % slow
        return remote(fit.at[group * fast + to], rec_y.at[e - 1, d - 1], y_s.at[e - 1, d - 1], y_r.at[e - 1, d - 1], grid=a * fast + to)

    width = fast * npp * vec
    for d in range(1, slow + 1):
        group = (a + d) % slow
        for i in range(fast * npp):
            hi, lo = split(x8b[group * (fast * npp) + i] * core_ref[...])
            vhi[group, :, i * vec:(i + 1) * vec] = hi
            vlo[group, :, i * vec:(i + 1) * vec] = lo
        part = dot3((xhi[...], xlo[...]), (vhi[group], vlo[group]), ((1,), (0,)))
        for i in range(fast * npp):
            fit[group * fast + i // npp, i % npp] = part[:, i * vec:(i + 1) * vec]
        for e in range(1, fast):
            y_copy(d, e).start()

    def z_copy(d):
        return remote(sum_y.at[d - 1], rec_z.at[d - 1], z_s.at[d - 1], z_r.at[d - 1], grid=((a + d) % slow) * fast + b)

    for d in range(1, slow + 1):
        group = (a + d) % slow
        acc = fit[group * fast + b]
        for e in range(1, fast):
            y_copy(d, e).wait_recv()
            acc = acc + rec_y[e - 1, d - 1]
        sum_y[d - 1] = acc
        if d < slow:
            z_copy(d).start()

    @pl.when(r != owner)
    def _():
        c_copy(1).wait_recv()

    acc = sum_y[slow - 1]
    for d in range(1, slow):
        z_copy(d).wait_recv()
        acc = acc + rec_z[d - 1]
    resid[j] = cbuf[...] - acc

    def gz_copy(d):
        return remote(resid.at[j], resid.at[j], gz_s.at[d - 1], gz_r.at[d - 1], grid=((a + d) % slow) * fast + b)

    def gy_copy(d, e):
        piece = ((a + slow - d) % slow) * fast + b
        return remote(resid.at[piece], resid.at[piece], gy_s.at[e - 1, d], gy_r.at[e - 1, d], grid=a * fast + (b + e) % fast)

    def p_copy(d, e):
        piece = ((a + slow - d) % slow) * fast + (b + fast - e) % fast
        keeps = piece // per_row
        return keeps, remote(resid.at[piece], res_ref.at[piece % per_row, r], p_s.at[d, e], p_r.at[piece % per_row, r], row=keeps), pltpu.make_async_copy(resid.at[piece], res_ref.at[piece % per_row, r], p_s.at[d, e])

    def to_keeper(d, e):
        keeps, far, near = p_copy(d, e)

        @pl.when(keeps != r)
        def _():
            far.start()

        @pl.when(keeps == r)
        def _():
            near.start()

    for d in range(1, slow):
        gz_copy(d).start()
    for e in range(1, fast):
        gy_copy(0, e).start()
    to_keeper(0, 0)

    outer[...] = jnp.zeros_like(outer)
    cg[...] = jnp.zeros_like(cg)
    cols[...] = jnp.zeros_like(cols)
    lane = lax.broadcasted_iota(jnp.int32, (pts, vec), 1)
    for d in range(slow):
        if d + 1 < slow:
            gz_copy(d + 1).wait_recv()
            for e in range(1, fast):
                gy_copy(d + 1, e).start()
            to_keeper(d + 1, 0)
        for e in range(1, fast):
            gy_copy(d, e).wait_recv()
            to_keeper(d, e)
        group = (a + slow - d) % slow
        parts = [resid[group * fast + i // npp, i % npp] for i in range(fast * npp)]
        rs = split(jnp.concatenate(parts, axis=1))
        outer[...] += dot3(rs, (vhi[group], vlo[group]), ((1,), (1,)))
        w = dot3((xhi[...], xlo[...]), rs, ((0,), (0,)))
        for i in range(fast * npp):
            p = group * (fast * npp) + i
            wp = w[:, i * vec:(i + 1) * vec]
            cg[...] += x8b[p] * wp
            cols[...] += jnp.where(lane == p, jnp.sum(wp * core_ref[...], axis=1, keepdims=True), 0.0)

    odd = r % 2
    mate = r + 1 - 2 * odd
    k_copy = remote(cg.at[pl.ds((1 - odd) * half, half)], cg_core, k_s.at[0], k_r.at[0], row=mate)
    k_copy.start()

    inner[...] = jnp.transpose(cols[...])[0:np_all, :]

    def i_copy():
        return remote(inner, inner_rec.at[r - 1], i_s.at[0], i_r.at[r - 1], row=0)

    @pl.when(r != 0)
    def _():
        i_copy().start()

    k_copy.wait_recv()
    cg_half[...] = cg[pl.ds(odd * half, half), :] + cg_core[...]

    def h_copy(t):
        return remote(cg_half, cg_row.at[t - 1], h_s.at[t - 1], h_r.at[t - 1], row=(r + 2 * t) % nrow)

    for t in range(1, nrow // 2):
        h_copy(t).start()

    fg_ref[...] = fg_scale * outer[0:rows, :]

    @pl.when(r == 0)
    def _():
        acc = outer[0:np_all, :] + inner[...]
        for e in range(1, nrow):
            remote(inner, inner_rec.at[e - 1], i_s.at[0], i_r.at[e - 1], row=e).wait_recv()
            acc = acc + inner_rec[e - 1]
        fg_ref[0:np_all, :] = fg_scale * acc

    acc = cg_half[...]
    for t in range(1, nrow // 2):
        h_copy(t).wait_recv()
        acc = acc + cg_row[t - 1]
    cg_fin[odd] = cg_scale * acc
    f_copy = remote(cg_fin.at[odd], cg_fin.at[odd], f_s.at[0], f_r.at[0], row=mate)
    f_copy.start()
    cg_ref[pl.ds(odd * half, half), :] = cg_fin[odd]
    f_copy.wait_recv()
    cg_ref[pl.ds((1 - odd) * half, half), :] = cg_fin[1 - odd]

    for t in range(per_row):
        for e in range(1, nrow):
            far = (r + e) % nrow
            remote(resid.at[0], res_ref.at[t, far], p_s.at[0, 0], p_r.at[t, far], row=far).wait_recv()
    for d in range(slow):
        for e in range(fast):
            keeps, far, near = p_copy(d, e)

            @pl.when(keeps != r)
            def _():
                far.wait_send()

            @pl.when(keeps == r)
            def _():
                near.wait()

    @pl.when(r == 0)
    def _():
        for e in range(1, nrow):
            x8_copy(e).wait_send()

    @pl.when(r == owner)
    def _():
        for e in range(1, nrow):
            c_copy(e).wait_send()

    @pl.when(r != 0)
    def _():
        i_copy().wait_send()

    for e in range(1, fast):
        for d in range(slow):
            y_copy(d + 1, e).wait_send()
            gy_copy(d, e).wait_send()
    for d in range(1, slow):
        z_copy(d).wait_send()
        gz_copy(d).wait_send()
    for t in range(1, nrow // 2):
        h_copy(t).wait_send()
    k_copy.wait_send()
    f_copy.wait_send()


def per_device(nrow, ngrid, cholesky, factor, core):
    held = cholesky.shape[0]
    rows, pts = factor.shape
    vec = core.shape[1]
    np_all = held * nrow
    npp = np_all // ngrid
    per_row = held // npp
    slow, fast = two_factors(ngrid)
    rpad = -(-rows // 16) * 16
    cg_scale = -1.0 / math.sqrt(np_all * rows * nrow)
    fg_scale = -math.sqrt(pts * ngrid / (rows * nrow * vec))
    cfg = (nrow, slow, fast, npp, rows, rpad, vec, cg_scale, fg_scale)

    slab = cholesky.reshape(held, nrow, rows, vec)
    slab = lax.dynamic_slice_in_dim(slab, (lax.axis_index("grid") % per_row) * npp, npp, 0)
    slab = jnp.pad(jnp.swapaxes(slab, 0, 1), ((0, 0), (0, 0), (0, rpad - rows), (0, 0)))

    piece = (npp, rpad, vec)
    dma = pltpu.SemaphoreType.DMA
    vmem = pl.BlockSpec(memory_space=pltpu.VMEM)
    width = fast * npp * vec
    scratch = [
        pltpu.VMEM((rpad, pts), F32), pltpu.VMEM((rpad, pts), BF16), pltpu.VMEM((rpad, pts), BF16),
        pltpu.VMEM((np_all, pts), F32), pltpu.VMEM((np_all, pts, vec), F32),
        pltpu.VMEM((slow, pts, width), BF16), pltpu.VMEM((slow, pts, width), BF16),
        pltpu.VMEM((ngrid,) + piece, F32),
        pltpu.VMEM((max(fast - 1, 1), slow) + piece, F32), pltpu.VMEM((slow,) + piece, F32),
        pltpu.VMEM((max(slow - 1, 1),) + piece, F32), pltpu.VMEM(piece, F32),
        pltpu.VMEM((ngrid,) + piece, F32),
        pltpu.VMEM((rpad, pts), F32), pltpu.VMEM((pts, vec), F32), pltpu.VMEM((pts, vec), F32),
        pltpu.VMEM((pts // 2, vec), F32), pltpu.VMEM((pts // 2, vec), F32),
        pltpu.VMEM((max(nrow // 2 - 1, 1), pts // 2, vec), F32), pltpu.VMEM((2, pts // 2, vec), F32),
        pltpu.VMEM((np_all, pts), F32), pltpu.VMEM((nrow - 1, np_all, pts), F32),
        dma((nrow - 1,)), dma((1,)), dma((nrow - 1,)), dma((1,)),
        dma((max(fast - 1, 1), slow)), dma((max(fast - 1, 1), slow)), dma((max(slow - 1, 1),)), dma((max(slow - 1, 1),)),
        dma((max(slow - 1, 1),)), dma((max(slow - 1, 1),)), dma((max(fast - 1, 1), slow)), dma((max(fast - 1, 1), slow)),
        dma((slow, fast)), dma((per_row, nrow)), dma((1,)), dma((nrow - 1,)),
        dma((1,)), dma((1,)), dma((max(nrow // 2 - 1, 1),)), dma((max(nrow // 2 - 1, 1),)), dma((1,)), dma((1,)),
    ]
    macs = 3 * rows * pts * np_all * vec
    res, cg, fg = pl.pallas_call(
        functools.partial(kernel, cfg),
        out_shape=(
            jax.ShapeDtypeStruct((per_row, nrow) + piece, F32),
            jax.ShapeDtypeStruct((pts, vec), F32),
            jax.ShapeDtypeStruct((rows, pts), F32),
        ),
        in_specs=[vmem] * 3,
        out_specs=(pl.BlockSpec(memory_space=pl.ANY), vmem, vmem),
        scratch_shapes=scratch,
        cost_estimate=pl.CostEstimate(flops=6 * macs, bytes_accessed=8 * rows * pts, transcendentals=0),
        compiler_params=pltpu.CompilerParams(collective_id=0, has_side_effects=True, vmem_limit_bytes=44 * 2**20),
        name="hypercontraction",
    )(factor, core, slab)
    res = jnp.swapaxes(res[:, :, :, :rows], 1, 2).reshape(held, nrow * rows * vec)
    return res, cg, fg


def solution(mesh):
    placed = (P("row", None), P("row", "grid"), P("grid", None))
    return jax.shard_map(
        functools.partial(per_device, mesh.shape["row"], mesh.shape["grid"]),
        mesh=mesh,
        in_specs=placed,
        out_specs=(P("row", None), P("grid", None), P("row", "grid")),
        check_vma=False,
    )
```

time: 248 us -> 72.6 us (0.29)
  the two profiles are of different devices: /device:TPU:0 before, /device:TPU:25 now
where the time goes in v1:
time: 72.6 us; the launch traced here: 72.4 us
  Pallas kernels  64.7 us (89%)
  local copies, waits for them, and re-layouts  7.05 us (10%)
    pallas_call x1, Pallas kernels, per_device(): pl.pallas_call(functools.partial(kernel, cfg), out_shape=(jax.ShapeDtypeS...  64.7 us
    unnamed x6, local copies, waits for them, and re-layouts  2.83 us
    reshape x1, local copies, waits for them, and re-layouts, per_device(): slab = cholesky.reshape(held, nrow, rows, vec)  2.34 us
    another operation x1, local copies, waits for them, and re-layouts, per_device(): jnp.swapaxes(res[:, :, :, :rows], 1, 2).reshape(held, nrow * rows * vec)  1.79 us

profile of v1, /device:TPU:25, one launch (start us, length us, event | category | flops | bytes accessed | tf_op | source)
XLA Modules:
  0.0 72.4 jit_solution(11390690634026630998)
XLA Ops:
  0.6 2.3 %reshape.9 = f32[2,4,300,128]{3,2,1,0:T(8,128)S(1)} reshape(f32[2,153600]{1,0:T(2,128)} %param.3) | data formatting | bytes 2457600 | tf_op jit(solution)/shard_map/reshape | solution.py:284
  3.0 0.0 copy-start
  3.0 0.0 copy-start.1
  3.0 0.1 dynamic-slice_bitcast_fusion
  3.1 1.1 %copy-done = f32[300,768]{1,0:T(8,128)S(1)} copy-done((f32[300,768]{1,0:T(8,128)S(1)}, f32[300,768]{1,0:T(8,128)}, u32[]{:S(2)}) %copy-start) | copy-done | bytes 921624
  4.2 0.1 copy-done.1
  4.3 64.7 %hypercontraction.1 = (f32[2,4,1,304,128]{4,3,2,1,0:T(8,128)S(1)}, f32[768,128]{1,0:T(8,128)S(1)}, f32[300,768]{1,0:T(8,128)S(1)}) custom-call(f32[300,768]{1,0:T(8,128)S(1)} %copy-done, f32[768,128]{1,0:T(8,128)S(1)} %copy-done.1, f32[4,1,304,128]{3,2,1,0:T(8,128)S(1)} %pad.4.chol_ref), custom_call_target="tpu_custom_call" | custom-call | flops 4246732800 | bytes 1843200 | tf_op jit(solution)/shard_map/hypercontraction/pallas_call | solution.py:311
  69.0 1.8 %reshape_transpose.3 = f32[2,153600]{1,0:T(2,128)} reshape(f32[2,4,1,300,128]{4,3,2,1,0:T(8,128)S(1)} %bitcast.3) | data formatting | bytes 2457600 | tf_op jit(solution)/shard_map/reshape;transpose | solution.py:325
  70.7 0.7 %copy.8 = f32[768,128]{1,0:T(8,128)} copy(f32[768,128]{1,0:T(8,128)S(1)} %get-tuple-element.13) | data formatting | bytes 786432
  71.5 0.9 %copy.9 = f32[300,768]{1,0:T(8,128)} copy(f32[300,768]{1,0:T(8,128)S(1)} %get-tuple-element.14) | data formatting | bytes 1843200
  (1 shorter events, 0.0 us)
Async XLA Ops:
  3.0 1.2 %copy-start = (f32[300,768]{1,0:T(8,128)S(1)}, f32[300,768]{1,0:T(8,128)}, u32[]{:S(2)}) copy-start(f32[300,768]{1,0:T(8,128)} %x_ref.1) | copy-start | bytes 2764804
  3.0 1.3 %copy-start.1 = (f32[768,128]{1,0:T(8,128)S(1)}, f32[768,128]{1,0:T(8,128)}, u32[]{:S(2)}) copy-start(f32[768,128]{1,0:T(8,128)} %core_ref.1) | copy-start | bytes 1179652

commit v2 on v1

v2 whole, which is shorter than its diff:
```python
import functools
import math

import jax
import jax.numpy as jnp
from jax import lax
from jax.experimental import pallas as pl
from jax.experimental.pallas import tpu as pltpu
from jax.sharding import PartitionSpec as P

MESH = pl.DeviceIdType.MESH
F32 = jnp.float32
BF16 = jnp.bfloat16


def split(x):
    hi = x.astype(BF16)
    return hi, (x - hi.astype(F32)).astype(BF16)


def dot3(left, right, dims):
    one = functools.partial(lax.dot_general, dimension_numbers=(dims, ((), ())), preferred_element_type=F32)
    return one(left[0], right[0]) + (one(left[0], right[1]) + one(left[1], right[0]))


def low_bit(m, bits):
    return next((s for s in range(bits) if m >> s & 1), bits)


def mirrored(m, bits):
    return sum((m >> s & 1) << (bits - 1 - s) for s in range(bits))


def kernel(cfg, x_hbm, core_hbm, chol_hbm, res_ref, cg_ref, fg_ref,
           xraw, xpad, core_ref, chol, xhi, xlo, x8, x8b, vhi, vlo, fit, rec, csend, cbuf, resid, prec, outer, cg, cols,
           cg_core, cg_half, cg_row, cg_fin, inner, inner_rec,
           in_s, x8_s, x8_r, c_s, c_r, rs_s, rs_r, ag_s, ag_r, p_s, p_r, i_s, i_r, k_s, k_r, h_s, h_r, f_s, f_r):
    nrow, bits, npp, held, rows, rpad, vec, chunks, cg_scale, fg_scale = cfg
    ngrid = 1 << bits
    np_all = npp * ngrid
    per_row = held // npp
    pts = x_hbm.shape[1]
    half = pts // 2
    r = lax.axis_index("row")
    j = lax.axis_index("grid")
    flips = [(1 - 2 * ((j // (1 << s)) % 2)) * (1 << s) for s in range(bits)]
    owner = j // per_row
    spans = [pl.ds(at, size) for at, size in chunks]

    def at(m):
        return j + sum(flips[s] for s in range(bits) if m >> s & 1)

    def remote(src, dst, ssem, rsem, **device):
        return pltpu.make_async_remote_copy(src_ref=src, dst_ref=dst, send_sem=ssem, recv_sem=rsem, device_id=device, device_id_type=MESH)

    x_in = pltpu.make_async_copy(x_hbm, xraw, in_s.at[0])
    core_in = pltpu.make_async_copy(core_hbm, core_ref, in_s.at[1])
    chol_in = pltpu.make_async_copy(chol_hbm, chol, in_s.at[2])
    x_in.start()
    core_in.start()
    chol_in.start()

    barrier = pltpu.get_barrier_semaphore()
    for e in range(1, nrow):
        pl.semaphore_signal(barrier, inc=1, device_id={"row": (r + e) % nrow}, device_id_type=MESH)
    for s in range(bits):
        pl.semaphore_signal(barrier, inc=1, device_id={"grid": at(1 << s)}, device_id_type=MESH)
    x_in.wait()
    pl.semaphore_wait(barrier, nrow - 1 + bits)

    def x8_copy(e):
        return remote(x8, x8, x8_s.at[e - 1], x8_r.at[0], row=(r + e) % nrow)

    def c_copy(e):
        to = (r + e) % nrow
        return remote(csend.at[to], cbuf, c_s.at[e - 1], c_r.at[0], row=to)

    @pl.when(r == 0)
    def _():
        x8[...] = xraw[0:np_all, :]
        for e in range(1, nrow):
            x8_copy(e).start()

    if rpad > rows:
        xpad[rows:rpad, :] = jnp.zeros((rpad - rows, pts), F32)
    xpad[0:rows, :] = xraw[...]
    hi, lo = split(xpad[...])
    xhi[...] = hi
    xlo[...] = lo
    chol_in.wait()
    for t in range(per_row):
        @pl.when((r == owner) & (j % per_row == t))
        def _():
            for to in range(nrow):
                for i in range(npp):
                    if rpad > rows:
                        csend[to, i, rows:rpad, :] = jnp.zeros((rpad - rows, vec), F32)
                    csend[to, i, 0:rows, :] = chol[pl.ds(to * rows * held + t * npp + i, rows, stride=held), :]

    @pl.when(r == owner)
    def _():
        for e in range(1, nrow):
            c_copy(e).start()
        cbuf[...] = csend[r]

    core_in.wait()

    @pl.when(r != 0)
    def _():
        x8_copy(1).wait_recv()

    flip = jnp.transpose(jnp.concatenate([x8[...], jnp.zeros((vec - np_all, pts), F32)], axis=0))
    for p in range(np_all):
        x8b[p] = jnp.broadcast_to(flip[:, p:p + 1], (pts, vec))

    slots = {}
    for s in range(bits):
        for m in range(0, ngrid, 2 << s):
            slots[s, m] = len(slots)

    def rs_copy(c, s, m):
        slot = slots[s, m ^ 1 << s]
        return remote(fit.at[at(m), :, spans[c]], rec.at[slot, :, spans[c]], rs_s.at[c, slot], rs_r.at[c, slot], grid=at(1 << s))

    down = sorted(range(ngrid), key=lambda m: -mirrored(m, bits))
    up = down[::-1]
    width = npp * vec
    for c, span in enumerate(spans):
        for first in range(0, ngrid, 2):
            two = down[first:first + 2]
            if c == 0:
                for m in two:
                    for i in range(npp):
                        hi, lo = split(x8b[at(m) * npp + i] * core_ref[...])
                        vhi[at(m), :, i * vec:(i + 1) * vec] = hi
                        vlo[at(m), :, i * vec:(i + 1) * vec] = lo
            v = [jnp.concatenate([buf[at(m)] for m in two], axis=1) for buf in (vhi, vlo)]
            part = dot3((xhi[span, :], xlo[span, :]), v, ((1,), (0,)))
            for n, m in enumerate(two):
                for i in range(npp):
                    fit[at(m), i, span, :] = part[:, n * width + i * vec:n * width + (i + 1) * vec]
                if m % 2:
                    rs_copy(c, 0, m).start()

    def ag_copy(c, s, m):
        return remote(resid.at[at(m), :, spans[c]], resid.at[at(m), :, spans[c]], ag_s.at[c, m + (1 << s)], ag_r.at[c, m + (1 << s)], grid=at(1 << s))

    def ag_wait(c, m):
        s = low_bit(m, bits)
        remote(resid.at[at(m), :, spans[c]], resid.at[at(m), :, spans[c]], ag_s.at[c, m], ag_r.at[c, m], grid=at(1 << s)).wait_recv()

    def p_copy(c, m):
        piece = at(m)
        keeps = piece // per_row
        src, dst = resid.at[piece, :, spans[c]], prec.at[piece % per_row, r, :, spans[c]]
        return keeps, remote(src, dst, p_s.at[c, m], p_r.at[c, piece % per_row, r], row=keeps), pltpu.make_async_copy(src, dst, p_s.at[c, m])

    def pass_on(c, m):
        for s in reversed(range(low_bit(m, bits))):
            ag_copy(c, s, m).start()
        keeps, far, near = p_copy(c, m)

        @pl.when(keeps != r)
        def _():
            far.start()

        @pl.when(keeps == r)
        def _():
            near.start()

    def reduce(c, m):
        for s in range(low_bit(m, bits)):
            rs_copy(c, s, m | 1 << s).wait_recv()
            fit[at(m), :, spans[c], :] += rec[slots[s, m], :, spans[c], :]
        if m:
            rs_copy(c, low_bit(m, bits), m).start()
            return
        if c == 0:
            @pl.when(r != owner)
            def _():
                c_copy(1).wait_recv()
        resid[j, :, spans[c], :] = cbuf[:, spans[c], :] - fit[j, :, spans[c], :]
        pass_on(c, 0)

    def arrive(c, m):
        ag_wait(c, m)
        pass_on(c, m)

    lane = lax.broadcasted_iota(jnp.int32, (pts, vec), 1)

    def gradient(c, first):
        two = up[first:first + 2]
        span = spans[c]
        rs = split(jnp.concatenate([resid[at(m), i, span, :] for m in two for i in range(npp)], axis=1))
        v = [jnp.concatenate([buf[at(m)] for m in two], axis=1) for buf in (vhi, vlo)]
        out = dot3(rs, v, ((1,), (1,)))
        outer[span, :] = out if first == 0 else outer[span, :] + out
        w = dot3((xhi[span, :], xlo[span, :]), rs, ((0,), (0,)))
        add_cg, add_cols = None, None
        for n, m in enumerate(two):
            for i in range(npp):
                p = at(m) * npp + i
                wp = w[:, n * width + i * vec:n * width + (i + 1) * vec]
                one = x8b[p] * wp
                col = jnp.where(lane == p, jnp.sum(wp * core_ref[...], axis=1, keepdims=True), 0.0)
                add_cg = one if add_cg is None else add_cg + one
                add_cols = col if add_cols is None else add_cols + col
        if c == 0 and first == 0:
            cg[...] = add_cg
            cols[...] = add_cols
        else:
            cg[...] += add_cg
            cols[...] += add_cols

    evens = [m for m in down if m % 2 == 0]
    inner_up = [m for m in up if m and m % 2 == 0]
    last = len(spans) - 1
    for m in evens:
        reduce(0, m)
    for c in range(1, last + 1):
        todo = list(inner_up)
        for n, m in enumerate(evens):
            reduce(c, m)
            if n >= len(evens) // 2 - 1 and m:
                for _ in range(2 if n == len(evens) // 2 - 1 else 1):
                    if todo:
                        arrive(c - 1, todo.pop(0))
        for m in todo:
            arrive(c - 1, m)
        odd_up = [m for m in up if m % 2]
        for n, m in enumerate(odd_up):
            arrive(c - 1, m)
            if n == len(odd_up) // 2 - 1:
                gradient(c - 1, 0)
        if c < last:
            for first in range(2, ngrid, 2):
                gradient(c - 1, first)
    pending = [(last - 1, first) for first in range(2, ngrid, 2)] if last else []
    for m in inner_up:
        arrive(last, m)
        if pending:
            gradient(*pending.pop(0))
    while pending:
        gradient(*pending.pop(0))
    for first in range(0, ngrid // 2, 2):
        gradient(last, first)
    for first in range(ngrid // 2, ngrid, 2):
        for m in up[first:first + 2]:
            arrive(last, m)
        gradient(last, first)

    odd = r % 2
    mate = r + 1 - 2 * odd
    k_copy = remote(cg.at[pl.ds((1 - odd) * half, half)], cg_core, k_s.at[0], k_r.at[0], row=mate)
    k_copy.start()

    inner[...] = jnp.transpose(cols[...])[0:np_all, :]

    def i_copy():
        return remote(inner, inner_rec.at[r - 1], i_s.at[0], i_r.at[r - 1], row=0)

    @pl.when(r != 0)
    def _():
        i_copy().start()

    k_copy.wait_recv()
    cg_half[...] = cg[pl.ds(odd * half, half), :] + cg_core[...]

    def h_copy(t):
        return remote(cg_half, cg_row.at[t - 1], h_s.at[t - 1], h_r.at[t - 1], row=(r + 2 * t) % nrow)

    for t in range(1, nrow // 2):
        h_copy(t).start()

    fg_ref[...] = fg_scale * outer[0:rows, :]

    @pl.when(r == 0)
    def _():
        acc = outer[0:np_all, :] + inner[...]
        for e in range(1, nrow):
            remote(inner, inner_rec.at[e - 1], i_s.at[0], i_r.at[e - 1], row=e).wait_recv()
            acc = acc + inner_rec[e - 1]
        fg_ref[0:np_all, :] = fg_scale * acc

    for c in range(len(spans)):
        for m in range(ngrid):
            keeps, far, near = p_copy(c, m)

            @pl.when(keeps != r)
            def _():
                far.wait_send()

            @pl.when(keeps == r)
            def _():
                near.wait()
    for src in range(nrow):
        @pl.when(r != src)
        def _():
            for t in range(per_row):
                for c, span in enumerate(spans):
                    here = prec.at[t, src, :, span]
                    remote(here, here, p_s.at[0, 0], p_r.at[c, t, src], row=src).wait_recv()

        for t in range(per_row):
            for i in range(npp):
                res_ref[pl.ds(src * rows * held + t * npp + i, rows, stride=held), :] = prec[t, src, i, 0:rows, :]

    acc = cg_half[...]
    for t in range(1, nrow // 2):
        h_copy(t).wait_recv()
        acc = acc + cg_row[t - 1]
    cg_fin[odd] = cg_scale * acc
    f_copy = remote(cg_fin.at[odd], cg_fin.at[odd], f_s.at[0], f_r.at[0], row=mate)
    f_copy.start()
    cg_ref[pl.ds(odd * half, half), :] = cg_fin[odd]
    f_copy.wait_recv()
    cg_ref[pl.ds((1 - odd) * half, half), :] = cg_fin[1 - odd]

    @pl.when(r == 0)
    def _():
        for e in range(1, nrow):
            x8_copy(e).wait_send()

    @pl.when(r == owner)
    def _():
        for e in range(1, nrow):
            c_copy(e).wait_send()

    @pl.when(r != 0)
    def _():
        i_copy().wait_send()

    for c in range(len(spans)):
        for s in range(bits):
            for m in range(0, ngrid, 2 << s):
                rs_copy(c, s, m | 1 << s).wait_send()
                ag_copy(c, s, m).wait_send()
    for t in range(1, nrow // 2):
        h_copy(t).wait_send()
    k_copy.wait_send()
    f_copy.wait_send()


def per_device(nrow, ngrid, cholesky, factor, core):
    held = cholesky.shape[0]
    rows, pts = factor.shape
    vec = core.shape[1]
    np_all = held * nrow
    npp = np_all // ngrid
    per_row = held // npp
    bits = ngrid.bit_length() - 1
    rpad = -(-rows // 16) * 16
    size = -(-rpad // 32) * 16
    chunks = [(0, size), (size, rpad - size)]
    cg_scale = -1.0 / math.sqrt(np_all * rows * nrow)
    fg_scale = -math.sqrt(pts * ngrid / (rows * nrow * vec))
    cfg = (nrow, bits, npp, held, rows, rpad, vec, chunks, cg_scale, fg_scale)

    slab = jnp.swapaxes(cholesky.reshape(held, nrow * rows, vec), 0, 1).reshape(nrow * rows * held, vec)

    piece = (npp, rpad, vec)
    nc = len(chunks)
    dma = pltpu.SemaphoreType.DMA
    vmem = pl.BlockSpec(memory_space=pltpu.VMEM)
    hbm = pl.BlockSpec(memory_space=pltpu.HBM)
    f32 = lambda *shape: pltpu.VMEM(shape, F32)
    b16 = lambda *shape: pltpu.VMEM(shape, BF16)
    pairs = max(nrow // 2 - 1, 1)
    scratch = [
        f32(rows, pts), f32(rpad, pts), f32(pts, vec), f32(nrow * rows * held, vec), b16(rpad, pts), b16(rpad, pts),
        f32(np_all, pts), f32(np_all, pts, vec),
        b16(ngrid, pts, npp * vec), b16(ngrid, pts, npp * vec),
        f32(ngrid, *piece), f32(ngrid - 1, *piece), f32(nrow, *piece), f32(*piece),
        f32(ngrid, *piece), f32(per_row, nrow, *piece),
        f32(rpad, pts), f32(pts, vec), f32(pts, vec),
        f32(pts // 2, vec), f32(pts // 2, vec), f32(pairs, pts // 2, vec), f32(2, pts // 2, vec),
        f32(np_all, pts), f32(nrow - 1, np_all, pts),
        dma((3,)), dma((nrow - 1,)), dma((1,)), dma((nrow - 1,)), dma((1,)),
        dma((nc, ngrid - 1)), dma((nc, ngrid - 1)), dma((nc, ngrid)), dma((nc, ngrid)),
        dma((nc, ngrid)), dma((nc, per_row, nrow)), dma((1,)), dma((nrow - 1,)),
        dma((1,)), dma((1,)), dma((pairs,)), dma((pairs,)), dma((1,)), dma((1,)),
    ]
    macs = 3 * rows * pts * np_all * vec
    res, cg, fg = pl.pallas_call(
        functools.partial(kernel, cfg),
        out_shape=(
            jax.ShapeDtypeStruct((nrow * rows * held, vec), F32),
            jax.ShapeDtypeStruct((pts, vec), F32),
            jax.ShapeDtypeStruct((rows, pts), F32),
        ),
        in_specs=[hbm] * 3,
        out_specs=(vmem, vmem, vmem),
        scratch_shapes=scratch,
        cost_estimate=pl.CostEstimate(flops=6 * macs, bytes_accessed=8 * rows * pts, transcendentals=0),
        compiler_params=pltpu.CompilerParams(collective_id=0, has_side_effects=True, vmem_limit_bytes=48 * 2**20),
        name="hypercontraction",
    )(factor, core, slab)
    res = jnp.swapaxes(res.reshape(nrow * rows, held, vec), 0, 1).reshape(held, nrow * rows * vec)
    return res, cg, fg


def solution(mesh):
    placed = (P("row", None), P("row", "grid"), P("grid", None))
    return jax.shard_map(
        functools.partial(per_device, mesh.shape["row"], mesh.shape["grid"]),
        mesh=mesh,
        in_specs=placed,
        out_specs=(P("row", None), P("grid", None), P("row", "grid")),
        check_vma=False,
    )
```

time: 72.6 us -> 65.2 us (0.90)
  the two profiles are of different devices: /device:TPU:25 before, /device:TPU:0 now
where the time goes in v2:
time: 65.2 us; the launch traced here: 65 us
  Pallas kernels  58.2 us (89%)
  local copies, waits for them, and re-layouts  6.16 us (9%)
    pallas_call x1, Pallas kernels, per_device(): pl.pallas_call(functools.partial(kernel, cfg), out_shape=(jax.ShapeDtypeS...  58.2 us
    unnamed x9, local copies, waits for them, and re-layouts  6.16 us

profile of v2, /device:TPU:0, one launch (start us, length us, event | category | flops | bytes accessed | tf_op | source)
XLA Modules:
  0.0 65.0 jit_solution(14775138370637568955)
XLA Ops:
  0.6 0.0 copy-start
  0.6 1.3 %copy-done = f32[2,153600]{1,0:T(2,128)S(1)} copy-done((f32[2,153600]{1,0:T(2,128)S(1)}, f32[2,153600]{1,0:T(2,128)}, u32[]{:S(2)}) %copy-start) | copy-done | bytes 1228824
  1.9 0.0 copy-start.1
  1.9 1.2 %copy-done.1 = f32[300,768]{1,0:T(8,128)S(1)} copy-done((f32[300,768]{1,0:T(8,128)S(1)}, f32[300,768]{1,0:T(8,128)}, u32[]{:S(2)}) %copy-start.1) | copy-done | bytes 921624
  3.1 0.0 copy-start.2
  3.1 1.0 %copy-done.2 = f32[768,128]{1,0:T(8,128)S(1)} copy-done((f32[768,128]{1,0:T(8,128)S(1)}, f32[768,128]{1,0:T(8,128)}, u32[]{:S(2)}) %copy-start.2) | copy-done | bytes 393240
  4.1 58.2 %hypercontraction.1 = (f32[2400,128]{1,0:T(8,128)S(1)}, f32[768,128]{1,0:T(8,128)S(1)}, f32[300,768]{1,0:T(8,128)S(1)}) custom-call(f32[300,768]{1,0:T(8,128)S(1)} %copy-done.1, f32[768,128]{1,0:T(8,128)S(1)} %copy-done.2, f32[2400,128]{1,0:T(8,128)S(1)} %bitcast.11), custom_call_target="tpu_custom_call" | custom-call | flops 4246732800 | bytes 1843200 | tf_op jit(solution)/shard_map/hypercontraction/pallas_call | solution.py:384
  62.3 1.0 %copy.11 = f32[2,153600]{1,0:T(2,128)} copy(f32[2,153600]{1,0:T(2,128)S(1)} %bitcast.10) | data formatting | bytes 2457600
  63.3 0.7 %copy.12 = f32[768,128]{1,0:T(8,128)} copy(f32[768,128]{1,0:T(8,128)S(1)} %get-tuple-element.13) | data formatting | bytes 786432
  64.1 0.9 %copy.13 = f32[300,768]{1,0:T(8,128)} copy(f32[300,768]{1,0:T(8,128)S(1)} %get-tuple-element.14) | data formatting | bytes 1843200
Async XLA Ops:
  0.6 1.3 %copy-start = (f32[2,153600]{1,0:T(2,128)S(1)}, f32[2,153600]{1,0:T(2,128)}, u32[]{:S(2)}) copy-start(f32[2,153600]{1,0:T(2,128)} %param.3) | copy-start | bytes 3686404
  1.9 1.2 %copy-start.1 = (f32[300,768]{1,0:T(8,128)S(1)}, f32[300,768]{1,0:T(8,128)}, u32[]{:S(2)}) copy-start(f32[300,768]{1,0:T(8,128)} %x_hbm.1) | copy-start | bytes 2764804
  3.1 1.0 %copy-start.2 = (f32[768,128]{1,0:T(8,128)S(1)}, f32[768,128]{1,0:T(8,128)}, u32[]{:S(2)}) copy-start(f32[768,128]{1,0:T(8,128)} %core_hbm.1) | copy-start | bytes 1179652

commit v3 on v2

--- a/solution.py
+++ b/solution.py
@@ -31,10 +31,11 @@
     return sum((m >> s & 1) << (bits - 1 - s) for s in range(bits))
 
 
-def kernel(cfg, x_hbm, core_hbm, chol_hbm, res_ref, cg_ref, fg_ref,
-           xraw, xpad, core_ref, chol, xhi, xlo, x8, x8b, vhi, vlo, fit, rec, csend, cbuf, resid, prec, outer, cg, cols,
+def kernel(cfg, x_hbm, core_hbm, chol_hbm, res_hbm, cg_hbm, fg_hbm,
+           xraw, xpad, core_ref, chol, xhi, xlo, x8, x8b, vhi, vlo, core_t, thi, tlo, fit, rec, csend, cbuf, resid, prec, outer, cg_t, cg,
+           res_ref, cg_ref, fg_ref,
            cg_core, cg_half, cg_row, cg_fin, inner, inner_rec,
-           in_s, x8_s, x8_r, c_s, c_r, rs_s, rs_r, ag_s, ag_r, p_s, p_r, i_s, i_r, k_s, k_r, h_s, h_r, f_s, f_r):
+           in_s, out_s, x8_s, x8_r, c_s, c_r, rs_s, rs_r, ag_s, ag_r, p_s, p_r, i_s, i_r, k_s, k_r, h_s, h_r, f_s, f_r):
     nrow, bits, npp, held, rows, rpad, vec, chunks, cg_scale, fg_scale = cfg
     ngrid = 1 << bits
     np_all = npp * ngrid
@@ -125,22 +126,23 @@
     down = sorted(range(ngrid), key=lambda m: -mirrored(m, bits))
     up = down[::-1]
     width = npp * vec
-    for c, span in enumerate(spans):
-        for first in range(0, ngrid, 2):
-            two = down[first:first + 2]
-            if c == 0:
-                for m in two:
-                    for i in range(npp):
-                        hi, lo = split(x8b[at(m) * npp + i] * core_ref[...])
-                        vhi[at(m), :, i * vec:(i + 1) * vec] = hi
-                        vlo[at(m), :, i * vec:(i + 1) * vec] = lo
-            v = [jnp.concatenate([buf[at(m)] for m in two], axis=1) for buf in (vhi, vlo)]
-            part = dot3((xhi[span, :], xlo[span, :]), v, ((1,), (0,)))
-            for n, m in enumerate(two):
+
+    def partial_fit(c, first):
+        span = spans[c]
+        two = down[first:first + 2]
+        if c == 0:
+            for m in two:
                 for i in range(npp):
-                    fit[at(m), i, span, :] = part[:, n * width + i * vec:n * width + (i + 1) * vec]
-                if m % 2:
-                    rs_copy(c, 0, m).start()
+                    hi, lo = split(x8b[at(m) * npp + i] * core_ref[...])
+                    vhi[at(m), :, i * vec:(i + 1) * vec] = hi
+                    vlo[at(m), :, i * vec:(i + 1) * vec] = lo
+        v = [jnp.concatenate([buf[at(m)] for m in two], axis=1) for buf in (vhi, vlo)]
+        part = dot3((xhi[span, :], xlo[span, :]), v, ((1,), (0,)))
+        for n, m in enumerate(two):
+            for i in range(npp):
+                fit[at(m), i, span, :] = part[:, n * width + i * vec:n * width + (i + 1) * vec]
+            if m % 2:
+                rs_copy(c, 0, m).start()
 
     def ag_copy(c, s, m):
         return remote(resid.at[at(m), :, spans[c]], resid.at[at(m), :, spans[c]], ag_s.at[c, m + (1 << s)], ag_r.at[c, m + (1 << s)], grid=at(1 << s))
@@ -186,37 +188,46 @@
         ag_wait(c, m)
         pass_on(c, m)
 
-    lane = lax.broadcasted_iota(jnp.int32, (pts, vec), 1)
-
     def gradient(c, first):
         two = up[first:first + 2]
         span = spans[c]
-        rs = split(jnp.concatenate([resid[at(m), i, span, :] for m in two for i in range(npp)], axis=1))
-        v = [jnp.concatenate([buf[at(m)] for m in two], axis=1) for buf in (vhi, vlo)]
-        out = dot3(rs, v, ((1,), (1,)))
+        piece = jnp.concatenate([resid[at(m), i, span, :] for m in two for i in range(npp)], axis=1)
+        t = [jnp.concatenate([buf[at(m)] for m in two], axis=0) for buf in (thi, tlo)]
+        out = dot3(split(piece), t, ((1,), (0,)))
         outer[span, :] = out if first == 0 else outer[span, :] + out
-        w = dot3((xhi[span, :], xlo[span, :]), rs, ((0,), (0,)))
-        add_cg, add_cols = None, None
+        w = dot3(split(jnp.transpose(piece)), (xhi[span, :], xlo[span, :]), ((1,), (0,)))
+        more = None
         for n, m in enumerate(two):
             for i in range(npp):
                 p = at(m) * npp + i
-                wp = w[:, n * width + i * vec:n * width + (i + 1) * vec]
-                one = x8b[p] * wp
-                col = jnp.where(lane == p, jnp.sum(wp * core_ref[...], axis=1, keepdims=True), 0.0)
-                add_cg = one if add_cg is None else add_cg + one
-                add_cols = col if add_cols is None else add_cols + col
-        if c == 0 and first == 0:
-            cg[...] = add_cg
-            cols[...] = add_cols
-        else:
-            cg[...] += add_cg
-            cols[...] += add_cols
+                wp = w[n * width + i * vec:n * width + (i + 1) * vec, :]
+                one = x8[pl.ds(p, 1), :] * wp
+                more = one if more is None else more + one
+                row = jnp.sum(wp * core_t[...], axis=0, keepdims=True)
+                inner[pl.ds(p, 1), :] = row if c == 0 else inner[pl.ds(p, 1), :] + row
+        cg_t[...] = more if c == 0 and first == 0 else cg_t[...] + more
 
     evens = [m for m in down if m % 2 == 0]
     inner_up = [m for m in up if m and m % 2 == 0]
     last = len(spans) - 1
-    for m in evens:
+    for first in range(0, ngrid, 2):
+        partial_fit(0, first)
+    for c in range(1, last + 1):
+        for first in range(0, ngrid // 2, 2):
+            partial_fit(c, first)
+    for m in evens[:len(evens) // 2]:
         reduce(0, m)
+    for c in range(1, last + 1):
+        for first in range(ngrid // 2, ngrid, 2):
+            partial_fit(c, first)
+    for m in evens[len(evens) // 2:-1]:
+        reduce(0, m)
+    core_t[...] = jnp.transpose(core_ref[...])
+    for p in range(np_all):
+        hi, lo = split(x8[p:p + 1, :] * core_t[...])
+        thi[p // npp, p % npp * vec:(p % npp + 1) * vec, :] = hi
+        tlo[p // npp, p % npp * vec:(p % npp + 1) * vec, :] = lo
+    reduce(0, 0)
     for c in range(1, last + 1):
         todo = list(inner_up)
         for n, m in enumerate(evens):
@@ -251,10 +262,9 @@
 
     odd = r % 2
     mate = r + 1 - 2 * odd
+    cg[...] = jnp.transpose(cg_t[...])
     k_copy = remote(cg.at[pl.ds((1 - odd) * half, half)], cg_core, k_s.at[0], k_r.at[0], row=mate)
     k_copy.start()
-
-    inner[...] = jnp.transpose(cols[...])[0:np_all, :]
 
     def i_copy():
         return remote(inner, inner_rec.at[r - 1], i_s.at[0], i_r.at[r - 1], row=0)
@@ -281,6 +291,9 @@
             remote(inner, inner_rec.at[e - 1], i_s.at[0], i_r.at[e - 1], row=e).wait_recv()
             acc = acc + inner_rec[e - 1]
         fg_ref[0:np_all, :] = fg_scale * acc
+
+    fg_out = pltpu.make_async_copy(fg_ref, fg_hbm, out_s.at[1])
+    fg_out.start()
 
     for c in range(len(spans)):
         for m in range(ngrid):
@@ -305,6 +318,9 @@
             for i in range(npp):
                 res_ref[pl.ds(src * rows * held + t * npp + i, rows, stride=held), :] = prec[t, src, i, 0:rows, :]
 
+    res_out = pltpu.make_async_copy(res_ref, res_hbm, out_s.at[0])
+    res_out.start()
+
     acc = cg_half[...]
     for t in range(1, nrow // 2):
         h_copy(t).wait_recv()
@@ -315,6 +331,8 @@
     cg_ref[pl.ds(odd * half, half), :] = cg_fin[odd]
     f_copy.wait_recv()
     cg_ref[pl.ds((1 - odd) * half, half), :] = cg_fin[1 - odd]
+    cg_out = pltpu.make_async_copy(cg_ref, cg_hbm, out_s.at[2])
+    cg_out.start()
 
     @pl.when(r == 0)
     def _():
@@ -339,6 +357,21 @@
         h_copy(t).wait_send()
     k_copy.wait_send()
     f_copy.wait_send()
+    res_out.wait()
+    fg_out.wait()
+    cg_out.wait()
+
+
+def hand_out(res_in, cg_in, fg_in, res_out, cg_out, fg_out, sems):
+    size = res_in.shape[0] // 4
+    copies = [pltpu.make_async_copy(src, dst, sems.at[n]) for n, (src, dst) in enumerate([(fg_in, fg_out), (cg_in, cg_out)])]
+    for n in range(4):
+        part = pl.ds(n * size, size)
+        copies.append(pltpu.make_async_copy(res_in.at[part], res_out.at[part], sems.at[2 + n]))
+    for copy in copies:
+        copy.start()
+    for copy in copies:
+        copy.wait()
 
 
 def per_device(nrow, ngrid, cholesky, factor, core):
@@ -361,7 +394,6 @@
     piece = (npp, rpad, vec)
     nc = len(chunks)
     dma = pltpu.SemaphoreType.DMA
-    vmem = pl.BlockSpec(memory_space=pltpu.VMEM)
     hbm = pl.BlockSpec(memory_space=pltpu.HBM)
     f32 = lambda *shape: pltpu.VMEM(shape, F32)
     b16 = lambda *shape: pltpu.VMEM(shape, BF16)
@@ -370,31 +402,42 @@
         f32(rows, pts), f32(rpad, pts), f32(pts, vec), f32(nrow * rows * held, vec), b16(rpad, pts), b16(rpad, pts),
         f32(np_all, pts), f32(np_all, pts, vec),
         b16(ngrid, pts, npp * vec), b16(ngrid, pts, npp * vec),
+        f32(vec, pts), b16(ngrid, npp * vec, pts), b16(ngrid, npp * vec, pts),
         f32(ngrid, *piece), f32(ngrid - 1, *piece), f32(nrow, *piece), f32(*piece),
         f32(ngrid, *piece), f32(per_row, nrow, *piece),
-        f32(rpad, pts), f32(pts, vec), f32(pts, vec),
+        f32(rpad, pts), f32(vec, pts), f32(pts, vec),
+        f32(nrow * rows * held, vec), f32(pts, vec), f32(rows, pts),
         f32(pts // 2, vec), f32(pts // 2, vec), f32(pairs, pts // 2, vec), f32(2, pts // 2, vec),
         f32(np_all, pts), f32(nrow - 1, np_all, pts),
-        dma((3,)), dma((nrow - 1,)), dma((1,)), dma((nrow - 1,)), dma((1,)),
+        dma((3,)), dma((3,)), dma((nrow - 1,)), dma((1,)), dma((nrow - 1,)), dma((1,)),
         dma((nc, ngrid - 1)), dma((nc, ngrid - 1)), dma((nc, ngrid)), dma((nc, ngrid)),
         dma((nc, ngrid)), dma((nc, per_row, nrow)), dma((1,)), dma((nrow - 1,)),
         dma((1,)), dma((1,)), dma((pairs,)), dma((pairs,)), dma((1,)), dma((1,)),
     ]
     macs = 3 * rows * pts * np_all * vec
-    res, cg, fg = pl.pallas_call(
+    results = (
+        jax.ShapeDtypeStruct((nrow * rows * held, vec), F32),
+        jax.ShapeDtypeStruct((pts, vec), F32),
+        jax.ShapeDtypeStruct((rows, pts), F32),
+    )
+    made = pl.pallas_call(
         functools.partial(kernel, cfg),
-        out_shape=(
-            jax.ShapeDtypeStruct((nrow * rows * held, vec), F32),
-            jax.ShapeDtypeStruct((pts, vec), F32),
-            jax.ShapeDtypeStruct((rows, pts), F32),
-        ),
+        out_shape=results,
         in_specs=[hbm] * 3,
-        out_specs=(vmem, vmem, vmem),
+        out_specs=(hbm, hbm, hbm),
         scratch_shapes=scratch,
         cost_estimate=pl.CostEstimate(flops=6 * macs, bytes_accessed=8 * rows * pts, transcendentals=0),
-        compiler_params=pltpu.CompilerParams(collective_id=0, has_side_effects=True, vmem_limit_bytes=48 * 2**20),
+        compiler_params=pltpu.CompilerParams(collective_id=0, has_side_effects=True, vmem_limit_bytes=62 * 2**20),
         name="hypercontraction",
     )(factor, core, slab)
+    res, cg, fg = pl.pallas_call(
+        hand_out,
+        out_shape=results,
+        in_specs=[pl.BlockSpec(memory_space=pl.ANY)] * 3,
+        out_specs=(hbm, hbm, hbm),
+        scratch_shapes=[dma((6,))],
+        name="hand_out",
+    )(*made)
     res = jnp.swapaxes(res.reshape(nrow * rows, held, vec), 0, 1).reshape(held, nrow * rows * vec)
     return res, cg, fg
 

time: 65.2 us -> 136 us (2.09)
  Pallas kernels: 58.2 us -> 136 us
  local copies, waits for them, and re-layouts: 6.16 us -> 0 us
    pallas_call x1 -> x2, Pallas kernels: 58.2 us -> 136 us  [the longest x1 78.6 us: per_device(): pl.pallas_call(hand_out, out_shape=results, in_specs=[pl.BlockSpec(memory...]
    unnamed x9 -> x0, local copies, waits for them, and re-layouts: 6.16 us -> none
where the time goes in v3:
time: 136 us
  Pallas kernels  136 us (100%)
    pallas_call x1, Pallas kernels, per_device(): pl.pallas_call(hand_out, out_shape=results, in_specs=[pl.BlockSpec(memory...  78.6 us
    pallas_call x1, Pallas kernels, per_device(): pl.pallas_call(functools.partial(kernel, cfg), out_shape=results, in_spec...  57.1 us

profile of v3, /device:TPU:0, one launch (start us, length us, event | category | flops | bytes accessed | tf_op | source)
XLA Modules:
  0.0 136.3 jit_solution(6052290011452741713)
XLA Ops:
  0.6 57.1 %hypercontraction.1 = (f32[2400,128]{1,0:T(8,128)}, f32[768,128]{1,0:T(8,128)}, f32[300,768]{1,0:T(8,128)}) custom-call(f32[300,768]{1,0:T(8,128)} %x_hbm.1, f32[768,128]{1,0:T(8,128)} %core_hbm.1, f32[2400,128]{1,0:T(8,128)} %bitcast.10), custom_call_target="tpu_custom_call" | custom-call | flops 4246732800 | bytes 1843200 | tf_op jit(solution)/shard_map/hypercontraction/pallas_call | solution.py:423
  57.7 78.6 %hand_out.1 = (f32[2400,128]{1,0:T(8,128)}, f32[768,128]{1,0:T(8,128)}, f32[300,768]{1,0:T(8,128)}) custom-call(f32[2400,128]{1,0:T(8,128)} %get-tuple-element.9.res_in, f32[768,128]{1,0:T(8,128)} %get-tuple-element.10.cg_in, f32[300,768]{1,0:T(8,128)} %get-tuple-element.11.fg_in), custom_call_target="tpu_custom_call" | custom-call | tf_op jit(solution)/shard_map/hand_out/pallas_call | solution.py:433

commit v4 on v3

--- a/solution.py
+++ b/solution.py
@@ -36,7 +36,7 @@
            res_ref, cg_ref, fg_ref,
            cg_core, cg_half, cg_row, cg_fin, inner, inner_rec,
            in_s, out_s, x8_s, x8_r, c_s, c_r, rs_s, rs_r, ag_s, ag_r, p_s, p_r, i_s, i_r, k_s, k_r, h_s, h_r, f_s, f_r):
-    nrow, bits, npp, held, rows, rpad, vec, chunks, cg_scale, fg_scale = cfg
+    nrow, bits, npp, held, rows, rpad, vec, chunks, orders, cg_scale, fg_scale = cfg
     ngrid = 1 << bits
     np_all = npp * ngrid
     per_row = held // npp
@@ -46,10 +46,14 @@
     j = lax.axis_index("grid")
     flips = [(1 - 2 * ((j // (1 << s)) % 2)) * (1 << s) for s in range(bits)]
     owner = j // per_row
-    spans = [pl.ds(at, size) for at, size in chunks]
-
-    def at(m):
-        return j + sum(flips[s] for s in range(bits) if m >> s & 1)
+    spans = [pl.ds(begin, size) for begin, size in chunks]
+    regions = [spans[0], pl.ds(chunks[1][0], rpad - chunks[1][0])]
+
+    def moved(c, m):
+        return sum(1 << orders[c][s] for s in range(bits) if m >> s & 1)
+
+    def at(c, m):
+        return j + sum(flips[s] for s in range(bits) if moved(c, m) >> s & 1)
 
     def remote(src, dst, ssem, rsem, **device):
         return pltpu.make_async_remote_copy(src_ref=src, dst_ref=dst, send_sem=ssem, recv_sem=rsem, device_id=device, device_id_type=MESH)
@@ -65,7 +69,7 @@
     for e in range(1, nrow):
         pl.semaphore_signal(barrier, inc=1, device_id={"row": (r + e) % nrow}, device_id_type=MESH)
     for s in range(bits):
-        pl.semaphore_signal(barrier, inc=1, device_id={"grid": at(1 << s)}, device_id_type=MESH)
+        pl.semaphore_signal(barrier, inc=1, device_id={"grid": at(0, 1 << s)}, device_id_type=MESH)
     x_in.wait()
     pl.semaphore_wait(barrier, nrow - 1 + bits)
 
@@ -121,38 +125,42 @@
 
     def rs_copy(c, s, m):
         slot = slots[s, m ^ 1 << s]
-        return remote(fit.at[at(m), :, spans[c]], rec.at[slot, :, spans[c]], rs_s.at[c, slot], rs_r.at[c, slot], grid=at(1 << s))
+        return remote(fit.at[at(c, m), :, spans[c]], rec.at[slot, :, spans[c]], rs_s.at[c, slot], rs_r.at[c, slot], grid=at(c, 1 << s))
 
     down = sorted(range(ngrid), key=lambda m: -mirrored(m, bits))
     up = down[::-1]
     width = npp * vec
-
-    def partial_fit(c, first):
-        span = spans[c]
+    late = []
+    for first in range(0, ngrid, 2):
         two = down[first:first + 2]
-        if c == 0:
-            for m in two:
-                for i in range(npp):
-                    hi, lo = split(x8b[at(m) * npp + i] * core_ref[...])
-                    vhi[at(m), :, i * vec:(i + 1) * vec] = hi
-                    vlo[at(m), :, i * vec:(i + 1) * vec] = lo
-        v = [jnp.concatenate([buf[at(m)] for m in two], axis=1) for buf in (vhi, vlo)]
-        part = dot3((xhi[span, :], xlo[span, :]), v, ((1,), (0,)))
+        for m in two:
+            for i in range(npp):
+                hi, lo = split(x8b[at(0, m) * npp + i] * core_ref[...])
+                vhi[at(0, m), :, i * vec:(i + 1) * vec] = hi
+                vlo[at(0, m), :, i * vec:(i + 1) * vec] = lo
+        v = [jnp.concatenate([buf[at(0, m)] for m in two], axis=1) for buf in (vhi, vlo)]
+        part = dot3((xhi[...], xlo[...]), v, ((1,), (0,)))
         for n, m in enumerate(two):
             for i in range(npp):
-                fit[at(m), i, span, :] = part[:, n * width + i * vec:n * width + (i + 1) * vec]
-            if m % 2:
-                rs_copy(c, 0, m).start()
+                fit[at(0, m), i] = part[:, n * width + i * vec:n * width + (i + 1) * vec]
+            for c in range(len(spans)):
+                own = next(o for o in range(ngrid) if moved(c, o) == m)
+                if own % 2 and c == 1:
+                    late.append(own)
+                elif own % 2:
+                    rs_copy(c, 0, own).start()
+    for own in late:
+        rs_copy(1, 0, own).start()
 
     def ag_copy(c, s, m):
-        return remote(resid.at[at(m), :, spans[c]], resid.at[at(m), :, spans[c]], ag_s.at[c, m + (1 << s)], ag_r.at[c, m + (1 << s)], grid=at(1 << s))
+        return remote(resid.at[at(c, m), :, spans[c]], resid.at[at(c, m), :, spans[c]], ag_s.at[c, m + (1 << s)], ag_r.at[c, m + (1 << s)], grid=at(c, 1 << s))
 
     def ag_wait(c, m):
         s = low_bit(m, bits)
-        remote(resid.at[at(m), :, spans[c]], resid.at[at(m), :, spans[c]], ag_s.at[c, m], ag_r.at[c, m], grid=at(1 << s)).wait_recv()
+        remote(resid.at[at(c, m), :, spans[c]], resid.at[at(c, m), :, spans[c]], ag_s.at[c, m], ag_r.at[c, m], grid=at(c, 1 << s)).wait_recv()
 
     def p_copy(c, m):
-        piece = at(m)
+        piece = at(c, m)
         keeps = piece // per_row
         src, dst = resid.at[piece, :, spans[c]], prec.at[piece % per_row, r, :, spans[c]]
         return keeps, remote(src, dst, p_s.at[c, m], p_r.at[c, piece % per_row, r], row=keeps), pltpu.make_async_copy(src, dst, p_s.at[c, m])
@@ -170,14 +178,18 @@
         def _():
             near.start()
 
+    ready = []
+
     def reduce(c, m):
         for s in range(low_bit(m, bits)):
             rs_copy(c, s, m | 1 << s).wait_recv()
-            fit[at(m), :, spans[c], :] += rec[slots[s, m], :, spans[c], :]
+            fit[at(c, m), :, spans[c], :] += rec[slots[s, m], :, spans[c], :]
         if m:
             rs_copy(c, low_bit(m, bits), m).start()
             return
-        if c == 0:
+        if not ready:
+            ready.append(c)
+
             @pl.when(r != owner)
             def _():
                 c_copy(1).wait_recv()
@@ -188,77 +200,48 @@
         ag_wait(c, m)
         pass_on(c, m)
 
-    def gradient(c, first):
+    def gradient(region, first):
         two = up[first:first + 2]
-        span = spans[c]
-        piece = jnp.concatenate([resid[at(m), i, span, :] for m in two for i in range(npp)], axis=1)
-        t = [jnp.concatenate([buf[at(m)] for m in two], axis=0) for buf in (thi, tlo)]
+        span = regions[region]
+        piece = jnp.concatenate([resid[at(0, m), i, span, :] for m in two for i in range(npp)], axis=1)
+        t = [jnp.concatenate([buf[at(0, m)] for m in two], axis=0) for buf in (thi, tlo)]
         out = dot3(split(piece), t, ((1,), (0,)))
         outer[span, :] = out if first == 0 else outer[span, :] + out
         w = dot3(split(jnp.transpose(piece)), (xhi[span, :], xlo[span, :]), ((1,), (0,)))
         more = None
         for n, m in enumerate(two):
             for i in range(npp):
-                p = at(m) * npp + i
+                p = at(0, m) * npp + i
                 wp = w[n * width + i * vec:n * width + (i + 1) * vec, :]
                 one = x8[pl.ds(p, 1), :] * wp
                 more = one if more is None else more + one
                 row = jnp.sum(wp * core_t[...], axis=0, keepdims=True)
-                inner[pl.ds(p, 1), :] = row if c == 0 else inner[pl.ds(p, 1), :] + row
-        cg_t[...] = more if c == 0 and first == 0 else cg_t[...] + more
+                inner[pl.ds(p, 1), :] = row if region == 0 else inner[pl.ds(p, 1), :] + row
+        cg_t[...] = more if region == 0 and first == 0 else cg_t[...] + more
 
     evens = [m for m in down if m % 2 == 0]
-    inner_up = [m for m in up if m and m % 2 == 0]
-    last = len(spans) - 1
-    for first in range(0, ngrid, 2):
-        partial_fit(0, first)
-    for c in range(1, last + 1):
-        for first in range(0, ngrid // 2, 2):
-            partial_fit(c, first)
-    for m in evens[:len(evens) // 2]:
-        reduce(0, m)
-    for c in range(1, last + 1):
-        for first in range(ngrid // 2, ngrid, 2):
-            partial_fit(c, first)
-    for m in evens[len(evens) // 2:-1]:
-        reduce(0, m)
+    lots = (evens, [m for m in up if m and m % 2 == 0], [m for m in up if m % 2])
+    expected = (((8.8, 14.7), (18.0, 21.3), (20.0, 24.6)), ((14.0, 20.0), (23.3, 26.6), (25.5, 30.0)), ((9.5, 15.0), (17.5, 21.0), (21.1, 23.0)))
+    when, events = {}, []
+    for c in range(len(spans)):
+        for kind, (lot, (begin, end)) in enumerate(zip(lots, expected[c])):
+            for n, m in enumerate(lot):
+                time = begin + (end - begin) * n / max(len(lot) - 1, 1)
+                when[c, kind > 0, moved(c, m)] = time
+                events.append((time, len(events), functools.partial(arrive if kind else reduce, c, m)))
+    for region, parts in enumerate(((0,), (1, 2))):
+        for first in range(0, ngrid, 2):
+            time = (22.2, 26.8)[region] + (6.0, 2.0)[region] * first / ngrid
+            time = max([time] + [when[c, m > 0, m] for c in parts for m in up[first:first + 2]])
+            events.append((time, len(events), functools.partial(gradient, region, first)))
+
     core_t[...] = jnp.transpose(core_ref[...])
     for p in range(np_all):
         hi, lo = split(x8[p:p + 1, :] * core_t[...])
         thi[p // npp, p % npp * vec:(p % npp + 1) * vec, :] = hi
         tlo[p // npp, p % npp * vec:(p % npp + 1) * vec, :] = lo
-    reduce(0, 0)
-    for c in range(1, last + 1):
-        todo = list(inner_up)
-        for n, m in enumerate(evens):
-            reduce(c, m)
-            if n >= len(evens) // 2 - 1 and m:
-                for _ in range(2 if n == len(evens) // 2 - 1 else 1):
-                    if todo:
-                        arrive(c - 1, todo.pop(0))
-        for m in todo:
-            arrive(c - 1, m)
-        odd_up = [m for m in up if m % 2]
-        for n, m in enumerate(odd_up):
-            arrive(c - 1, m)
-            if n == len(odd_up) // 2 - 1:
-                gradient(c - 1, 0)
-        if c < last:
-            for first in range(2, ngrid, 2):
-                gradient(c - 1, first)
-    pending = [(last - 1, first) for first in range(2, ngrid, 2)] if last else []
-    for m in inner_up:
-        arrive(last, m)
-        if pending:
-            gradient(*pending.pop(0))
-    while pending:
-        gradient(*pending.pop(0))
-    for first in range(0, ngrid // 2, 2):
-        gradient(last, first)
-    for first in range(ngrid // 2, ngrid, 2):
-        for m in up[first:first + 2]:
-            arrive(last, m)
-        gradient(last, first)
+    for _, _, event in sorted(events, key=lambda item: item[:2]):
+        event()
 
     odd = r % 2
     mate = r + 1 - 2 * odd
@@ -362,15 +345,20 @@
     cg_out.wait()
 
 
-def hand_out(res_in, cg_in, fg_in, res_out, cg_out, fg_out, sems):
+def hand_out(res_in, cg_in, fg_in, res_out, cg_out, fg_out, res, cg, fg, sems):
     size = res_in.shape[0] // 4
-    copies = [pltpu.make_async_copy(src, dst, sems.at[n]) for n, (src, dst) in enumerate([(fg_in, fg_out), (cg_in, cg_out)])]
+    ways = [(fg_in, fg, fg_out), (cg_in, cg, cg_out)]
     for n in range(4):
         part = pl.ds(n * size, size)
-        copies.append(pltpu.make_async_copy(res_in.at[part], res_out.at[part], sems.at[2 + n]))
-    for copy in copies:
+        ways.append((res_in.at[part], res.at[part], res_out.at[part]))
+    into = [pltpu.make_async_copy(src, mid, sems.at[0, n]) for n, (src, mid, _) in enumerate(ways)]
+    out = [pltpu.make_async_copy(mid, dst, sems.at[1, n]) for n, (_, mid, dst) in enumerate(ways)]
+    for copy in into:
         copy.start()
-    for copy in copies:
+    for first, second in zip(into, out):
+        first.wait()
+        second.start()
+    for copy in out:
         copy.wait()
 
 
@@ -383,11 +371,15 @@
     per_row = held // npp
     bits = ngrid.bit_length() - 1
     rpad = -(-rows // 16) * 16
-    size = -(-rpad // 32) * 16
-    chunks = [(0, size), (size, rpad - size)]
+    tiles = rpad // 16
+    third = max(1, tiles // 6)
+    sizes = [-(-(tiles - third) // 2) * 16, (tiles - third) // 2 * 16, third * 16]
+    chunks = [(sum(sizes[:n]), size) for n, size in enumerate(sizes)]
+    plain = list(range(bits))
+    orders = [plain, plain, plain[1:] + plain[:1]]
     cg_scale = -1.0 / math.sqrt(np_all * rows * nrow)
     fg_scale = -math.sqrt(pts * ngrid / (rows * nrow * vec))
-    cfg = (nrow, bits, npp, held, rows, rpad, vec, chunks, cg_scale, fg_scale)
+    cfg = (nrow, bits, npp, held, rows, rpad, vec, chunks, orders, cg_scale, fg_scale)
 
     slab = jnp.swapaxes(cholesky.reshape(held, nrow * rows, vec), 0, 1).reshape(nrow * rows * held, vec)
 
@@ -435,7 +427,7 @@
         out_shape=results,
         in_specs=[pl.BlockSpec(memory_space=pl.ANY)] * 3,
         out_specs=(hbm, hbm, hbm),
-        scratch_shapes=[dma((6,))],
+        scratch_shapes=[f32(nrow * rows * held, vec), f32(pts, vec), f32(rows, pts), dma((2, 6))],
         name="hand_out",
     )(*made)
     res = jnp.swapaxes(res.reshape(nrow * rows, held, vec), 0, 1).reshape(held, nrow * rows * vec)

time: 136 us -> 57.3 us (0.42)
  Pallas kernels: 136 us -> 56.5 us
    pallas_call x1, Pallas kernels: 78.6 us -> 2.75 us  [per_device(): pl.pallas_call(hand_out, out_shape=results, in_specs=[pl.BlockSpec(memory...]
    pallas_call x1, Pallas kernels: 57.1 us -> 53.7 us  [per_device(): pl.pallas_call(functools.partial(kernel, cfg), out_shape=results, in_spec...]
where the time goes in v4:
time: 57.3 us; the launch traced here: 57.1 us
  Pallas kernels  56.5 us (99%)
  between operations  0.64 us (1%)
    pallas_call x1, Pallas kernels, per_device(): pl.pallas_call(functools.partial(kernel, cfg), out_shape=results, in_spec...  53.7 us
    pallas_call x1, Pallas kernels, per_device(): pl.pallas_call(hand_out, out_shape=results, in_specs=[pl.BlockSpec(memory...  2.75 us

profile of v4, /device:TPU:0, one launch (start us, length us, event | category | flops | bytes accessed | tf_op | source)
XLA Modules:
  0.0 57.1 jit_solution(2931976703279724726)
XLA Ops:
  0.6 53.7 %hypercontraction.1 = (f32[2400,128]{1,0:T(8,128)}, f32[768,128]{1,0:T(8,128)}, f32[300,768]{1,0:T(8,128)}) custom-call(f32[300,768]{1,0:T(8,128)} %x_hbm.1, f32[768,128]{1,0:T(8,128)} %core_hbm.1, f32[2400,128]{1,0:T(8,128)} %bitcast.10), custom_call_target="tpu_custom_call" | custom-call | flops 4246732800 | bytes 1843200 | tf_op jit(solution)/shard_map/hypercontraction/pallas_call | solution.py:415
  54.4 2.7 %hand_out.1 = (f32[2400,128]{1,0:T(8,128)}, f32[768,128]{1,0:T(8,128)}, f32[300,768]{1,0:T(8,128)}) custom-call(f32[2400,128]{1,0:T(8,128)} %get-tuple-element.9.res_in, f32[768,128]{1,0:T(8,128)} %get-tuple-element.10.cg_in, f32[300,768]{1,0:T(8,128)} %get-tuple-element.11.fg_in), custom_call_target="tpu_custom_call" | custom-call | tf_op jit(solution)/shard_map/hand_out/pallas_call | solution.py:425

commit v5 on v4

--- a/solution.py
+++ b/solution.py
@@ -33,7 +33,7 @@
 
 def kernel(cfg, x_hbm, core_hbm, chol_hbm, res_hbm, cg_hbm, fg_hbm,
            xraw, xpad, core_ref, chol, xhi, xlo, x8, x8b, vhi, vlo, core_t, thi, tlo, fit, rec, csend, cbuf, resid, prec, outer, cg_t, cg,
-           res_ref, cg_ref, fg_ref,
+           res_ref, fg_ref,
            cg_core, cg_half, cg_row, cg_fin, inner, inner_rec,
            in_s, out_s, x8_s, x8_r, c_s, c_r, rs_s, rs_r, ag_s, ag_r, p_s, p_r, i_s, i_r, k_s, k_r, h_s, h_r, f_s, f_r):
     nrow, bits, npp, held, rows, rpad, vec, chunks, orders, cg_scale, fg_scale = cfg
@@ -47,7 +47,7 @@
     flips = [(1 - 2 * ((j // (1 << s)) % 2)) * (1 << s) for s in range(bits)]
     owner = j // per_row
     spans = [pl.ds(begin, size) for begin, size in chunks]
-    regions = [spans[0], pl.ds(chunks[1][0], rpad - chunks[1][0])]
+    regions = [pl.ds(0, chunks[1][0]), spans[1]]
 
     def moved(c, m):
         return sum(1 << orders[c][s] for s in range(bits) if m >> s & 1)
@@ -61,6 +61,12 @@
     x_in = pltpu.make_async_copy(x_hbm, xraw, in_s.at[0])
     core_in = pltpu.make_async_copy(core_hbm, core_ref, in_s.at[1])
     chol_in = pltpu.make_async_copy(chol_hbm, chol, in_s.at[2])
+    x8_in = pltpu.make_async_copy(x_hbm.at[pl.ds(0, np_all)], x8, in_s.at[3])
+
+    @pl.when(r == 0)
+    def _():
+        x8_in.start()
+
     x_in.start()
     core_in.start()
     chol_in.start()
@@ -70,7 +76,6 @@
         pl.semaphore_signal(barrier, inc=1, device_id={"row": (r + e) % nrow}, device_id_type=MESH)
     for s in range(bits):
         pl.semaphore_signal(barrier, inc=1, device_id={"grid": at(0, 1 << s)}, device_id_type=MESH)
-    x_in.wait()
     pl.semaphore_wait(barrier, nrow - 1 + bits)
 
     def x8_copy(e):
@@ -82,32 +87,17 @@
 
     @pl.when(r == 0)
     def _():
-        x8[...] = xraw[0:np_all, :]
+        x8_in.wait()
         for e in range(1, nrow):
             x8_copy(e).start()
 
+    x_in.wait()
     if rpad > rows:
         xpad[rows:rpad, :] = jnp.zeros((rpad - rows, pts), F32)
     xpad[0:rows, :] = xraw[...]
     hi, lo = split(xpad[...])
     xhi[...] = hi
     xlo[...] = lo
-    chol_in.wait()
-    for t in range(per_row):
-        @pl.when((r == owner) & (j % per_row == t))
-        def _():
-            for to in range(nrow):
-                for i in range(npp):
-                    if rpad > rows:
-                        csend[to, i, rows:rpad, :] = jnp.zeros((rpad - rows, vec), F32)
-                    csend[to, i, 0:rows, :] = chol[pl.ds(to * rows * held + t * npp + i, rows, stride=held), :]
-
-    @pl.when(r == owner)
-    def _():
-        for e in range(1, nrow):
-            c_copy(e).start()
-        cbuf[...] = csend[r]
-
     core_in.wait()
 
     @pl.when(r != 0)
@@ -131,6 +121,24 @@
     up = down[::-1]
     width = npp * vec
     late = []
+
+    def give_cholesky():
+        chol_in.wait()
+        for t in range(per_row):
+            @pl.when((r == owner) & (j % per_row == t))
+            def _():
+                for to in range(nrow):
+                    for i in range(npp):
+                        if rpad > rows:
+                            csend[to, i, rows:rpad, :] = jnp.zeros((rpad - rows, vec), F32)
+                        csend[to, i, 0:rows, :] = chol[pl.ds(to * rows * held + t * npp + i, rows, stride=held), :]
+
+        @pl.when(r == owner)
+        def _():
+            for e in range(1, nrow):
+                c_copy(e).start()
+            cbuf[...] = csend[r]
+
     for first in range(0, ngrid, 2):
         two = down[first:first + 2]
         for m in two:
@@ -149,6 +157,8 @@
                     late.append(own)
                 elif own % 2:
                     rs_copy(c, 0, own).start()
+        if first == 0:
+            give_cholesky()
     for own in late:
         rs_copy(1, 0, own).start()
 
@@ -229,7 +239,7 @@
                 time = begin + (end - begin) * n / max(len(lot) - 1, 1)
                 when[c, kind > 0, moved(c, m)] = time
                 events.append((time, len(events), functools.partial(arrive if kind else reduce, c, m)))
-    for region, parts in enumerate(((0,), (1, 2))):
+    for region, parts in enumerate(((0, 2), (1,))):
         for first in range(0, ngrid, 2):
             time = (22.2, 26.8)[region] + (6.0, 2.0)[region] * first / ngrid
             time = max([time] + [when[c, m > 0, m] for c in parts for m in up[first:first + 2]])
@@ -245,9 +255,16 @@
 
     odd = r % 2
     mate = r + 1 - 2 * odd
-    cg[...] = jnp.transpose(cg_t[...])
-    k_copy = remote(cg.at[pl.ds((1 - odd) * half, half)], cg_core, k_s.at[0], k_r.at[0], row=mate)
+    mine = pl.multiple_of(odd * half, half)
+    other = pl.multiple_of((1 - odd) * half, half)
+    if half % 128:
+        cg[...] = jnp.transpose(cg_t[...])
+    else:
+        cg[pl.ds(other, half), :] = jnp.transpose(cg_t[:, pl.ds(other, half)])
+    k_copy = remote(cg.at[pl.ds(other, half)], cg_core, k_s.at[0], k_r.at[0], row=mate)
     k_copy.start()
+    if half % 128 == 0:
+        cg[pl.ds(mine, half), :] = jnp.transpose(cg_t[:, pl.ds(mine, half)])
 
     def i_copy():
         return remote(inner, inner_rec.at[r - 1], i_s.at[0], i_r.at[r - 1], row=0)
@@ -257,13 +274,16 @@
         i_copy().start()
 
     k_copy.wait_recv()
-    cg_half[...] = cg[pl.ds(odd * half, half), :] + cg_core[...]
-
-    def h_copy(t):
-        return remote(cg_half, cg_row.at[t - 1], h_s.at[t - 1], h_r.at[t - 1], row=(r + 2 * t) % nrow)
-
-    for t in range(1, nrow // 2):
-        h_copy(t).start()
+    cg_half[...] = cg[pl.ds(mine, half), :] + cg_core[...]
+    block = half // 2
+
+    def h_copy(n, t):
+        part = pl.ds(n * block, block)
+        return remote(cg_half.at[part], cg_row.at[t - 1, part], h_s.at[n, t - 1], h_r.at[n, t - 1], row=(r + 2 * t) % nrow)
+
+    for n in range(2):
+        for t in range(1, nrow // 2):
+            h_copy(n, t).start()
 
     fg_ref[...] = fg_scale * outer[0:rows, :]
 
@@ -304,18 +324,22 @@
     res_out = pltpu.make_async_copy(res_ref, res_hbm, out_s.at[0])
     res_out.start()
 
-    acc = cg_half[...]
-    for t in range(1, nrow // 2):
-        h_copy(t).wait_recv()
-        acc = acc + cg_row[t - 1]
-    cg_fin[odd] = cg_scale * acc
-    f_copy = remote(cg_fin.at[odd], cg_fin.at[odd], f_s.at[0], f_r.at[0], row=mate)
-    f_copy.start()
-    cg_ref[pl.ds(odd * half, half), :] = cg_fin[odd]
-    f_copy.wait_recv()
-    cg_ref[pl.ds((1 - odd) * half, half), :] = cg_fin[1 - odd]
-    cg_out = pltpu.make_async_copy(cg_ref, cg_hbm, out_s.at[2])
-    cg_out.start()
+    def f_copy(n):
+        dst = cg_hbm.at[pl.ds(pl.multiple_of(odd * half + n * block, block), block)]
+        return remote(cg_fin.at[n], dst, f_s.at[n], f_r.at[n], row=mate), pltpu.make_async_copy(cg_fin.at[n], dst, out_s.at[2 + n])
+
+    for n in range(2):
+        part = pl.ds(n * block, block)
+        acc = cg_half[part, :]
+        for t in range(1, nrow // 2):
+            h_copy(n, t).wait_recv()
+            acc = acc + cg_row[t - 1, part, :]
+        cg_fin[n] = cg_scale * acc
+        for copy in f_copy(n):
+            copy.start()
+    for n in range(2):
+        here = cg_hbm.at[pl.ds(pl.multiple_of((1 - odd) * half + n * block, block), block)]
+        remote(cg_fin.at[n], here, f_s.at[n], f_r.at[n], row=mate).wait_recv()
 
     @pl.when(r == 0)
     def _():
@@ -336,21 +360,24 @@
             for m in range(0, ngrid, 2 << s):
                 rs_copy(c, s, m | 1 << s).wait_send()
                 ag_copy(c, s, m).wait_send()
-    for t in range(1, nrow // 2):
-        h_copy(t).wait_send()
+    for n in range(2):
+        for t in range(1, nrow // 2):
+            h_copy(n, t).wait_send()
+        far, near = f_copy(n)
+        far.wait_send()
+        near.wait()
     k_copy.wait_send()
-    f_copy.wait_send()
     res_out.wait()
     fg_out.wait()
-    cg_out.wait()
 
 
 def hand_out(res_in, cg_in, fg_in, res_out, cg_out, fg_out, res, cg, fg, sems):
-    size = res_in.shape[0] // 4
-    ways = [(fg_in, fg, fg_out), (cg_in, cg, cg_out)]
-    for n in range(4):
-        part = pl.ds(n * size, size)
-        ways.append((res_in.at[part], res.at[part], res_out.at[part]))
+    ways = []
+    for src, mid, dst, axis, parts in ((res_in, res, res_out, 0, 6), (fg_in, fg, fg_out, 1, 3), (cg_in, cg, cg_out, 0, 3)):
+        size = src.shape[axis] // parts
+        for n in range(parts):
+            part = (slice(None),) * axis + (pl.ds(n * size, size),)
+            ways.append((src.at[part], mid.at[part], dst.at[part]))
     into = [pltpu.make_async_copy(src, mid, sems.at[0, n]) for n, (src, mid, _) in enumerate(ways)]
     out = [pltpu.make_async_copy(mid, dst, sems.at[1, n]) for n, (_, mid, dst) in enumerate(ways)]
     for copy in into:
@@ -374,7 +401,7 @@
     tiles = rpad // 16
     third = max(1, tiles // 6)
     sizes = [-(-(tiles - third) // 2) * 16, (tiles - third) // 2 * 16, third * 16]
-    chunks = [(sum(sizes[:n]), size) for n, size in enumerate(sizes)]
+    chunks = [(0, sizes[0]), (sizes[0] + sizes[2], sizes[1]), (sizes[0], sizes[2])]
     plain = list(range(bits))
     orders = [plain, plain, plain[1:] + plain[:1]]
     cg_scale = -1.0 / math.sqrt(np_all * rows * nrow)
@@ -398,13 +425,13 @@
         f32(ngrid, *piece), f32(ngrid - 1, *piece), f32(nrow, *piece), f32(*piece),
         f32(ngrid, *piece), f32(per_row, nrow, *piece),
         f32(rpad, pts), f32(vec, pts), f32(pts, vec),
-        f32(nrow * rows * held, vec), f32(pts, vec), f32(rows, pts),
-        f32(pts // 2, vec), f32(pts // 2, vec), f32(pairs, pts // 2, vec), f32(2, pts // 2, vec),
+        f32(nrow * rows * held, vec), f32(rows, pts),
+        f32(pts // 2, vec), f32(pts // 2, vec), f32(pairs, pts // 2, vec), f32(2, pts // 4, vec),
         f32(np_all, pts), f32(nrow - 1, np_all, pts),
-        dma((3,)), dma((3,)), dma((nrow - 1,)), dma((1,)), dma((nrow - 1,)), dma((1,)),
+        dma((4,)), dma((4,)), dma((nrow - 1,)), dma((1,)), dma((nrow - 1,)), dma((1,)),
         dma((nc, ngrid - 1)), dma((nc, ngrid - 1)), dma((nc, ngrid)), dma((nc, ngrid)),
         dma((nc, ngrid)), dma((nc, per_row, nrow)), dma((1,)), dma((nrow - 1,)),
-        dma((1,)), dma((1,)), dma((pairs,)), dma((pairs,)), dma((1,)), dma((1,)),
+        dma((1,)), dma((1,)), dma((2, pairs)), dma((2, pairs)), dma((2,)), dma((2,)),
     ]
     macs = 3 * rows * pts * np_all * vec
     results = (
@@ -427,7 +454,7 @@
         out_shape=results,
         in_specs=[pl.BlockSpec(memory_space=pl.ANY)] * 3,
         out_specs=(hbm, hbm, hbm),
-        scratch_shapes=[f32(nrow * rows * held, vec), f32(pts, vec), f32(rows, pts), dma((2, 6))],
+        scratch_shapes=[f32(nrow * rows * held, vec), f32(pts, vec), f32(rows, pts), dma((2, 12))],
         name="hand_out",
     )(*made)
     res = jnp.swapaxes(res.reshape(nrow * rows, held, vec), 0, 1).reshape(held, nrow * rows * vec)

time: 57.3 us -> 57.8 us (level)
  no operation moved by 1% of the time
where the time goes in v5:
time: 57.8 us; the launch traced here: 57.6 us
  Pallas kernels  57 us (99%)
  between operations  0.64 us (1%)
    pallas_call x1, Pallas kernels, per_device(): pl.pallas_call(functools.partial(kernel, cfg), out_shape=results, in_spec...  54.3 us
    pallas_call x1, Pallas kernels, per_device(): pl.pallas_call(hand_out, out_shape=results, in_specs=[pl.BlockSpec(memory...  2.72 us

profile of v5, /device:TPU:0, one launch (start us, length us, event | category | flops | bytes accessed | tf_op | source)
XLA Modules:
  0.0 57.6 jit_solution(192704008391813023)
XLA Ops:
  0.6 54.3 %hypercontraction.1 = (f32[2400,128]{1,0:T(8,128)}, f32[768,128]{1,0:T(8,128)}, f32[300,768]{1,0:T(8,128)}) custom-call(f32[300,768]{1,0:T(8,128)} %x_hbm.1, f32[768,128]{1,0:T(8,128)} %core_hbm.1, f32[2400,128]{1,0:T(8,128)} %bitcast.10), custom_call_target="tpu_custom_call" | custom-call | flops 4246732800 | bytes 1843200 | tf_op jit(solution)/shard_map/hypercontraction/pallas_call | solution.py:442
  54.9 2.7 %hand_out.1 = (f32[2400,128]{1,0:T(8,128)}, f32[768,128]{1,0:T(8,128)}, f32[300,768]{1,0:T(8,128)}) custom-call(f32[2400,128]{1,0:T(8,128)} %get-tuple-element.9.res_in, f32[768,128]{1,0:T(8,128)} %get-tuple-element.10.cg_in, f32[300,768]{1,0:T(8,128)} %get-tuple-element.11.fg_in), custom_call_target="tpu_custom_call" | custom-call | tf_op jit(solution)/shard_map/hand_out/pallas_call | solution.py:452

commit v6 on v5

--- a/solution.py
+++ b/solution.py
@@ -47,7 +47,7 @@
     flips = [(1 - 2 * ((j // (1 << s)) % 2)) * (1 << s) for s in range(bits)]
     owner = j // per_row
     spans = [pl.ds(begin, size) for begin, size in chunks]
-    regions = [pl.ds(0, chunks[1][0]), spans[1]]
+    regions = [pl.ds(0, chunks[1][0]), pl.ds(chunks[1][0], rpad - chunks[1][0])]
 
     def moved(c, m):
         return sum(1 << orders[c][s] for s in range(bits) if m >> s & 1)
@@ -120,7 +120,7 @@
     down = sorted(range(ngrid), key=lambda m: -mirrored(m, bits))
     up = down[::-1]
     width = npp * vec
-    late = []
+    late = {1: [], 3: []}
 
     def give_cholesky():
         chol_in.wait()
@@ -153,14 +153,15 @@
                 fit[at(0, m), i] = part[:, n * width + i * vec:n * width + (i + 1) * vec]
             for c in range(len(spans)):
                 own = next(o for o in range(ngrid) if moved(c, o) == m)
-                if own % 2 and c == 1:
-                    late.append(own)
+                if own % 2 and c in late:
+                    late[c].append(own)
                 elif own % 2:
                     rs_copy(c, 0, own).start()
         if first == 0:
             give_cholesky()
-    for own in late:
-        rs_copy(1, 0, own).start()
+    for c, owns in late.items():
+        for own in owns:
+            rs_copy(c, 0, own).start()
 
     def ag_copy(c, s, m):
         return remote(resid.at[at(c, m), :, spans[c]], resid.at[at(c, m), :, spans[c]], ag_s.at[c, m + (1 << s)], ag_r.at[c, m + (1 << s)], grid=at(c, 1 << s))
@@ -231,7 +232,12 @@
 
     evens = [m for m in down if m % 2 == 0]
     lots = (evens, [m for m in up if m and m % 2 == 0], [m for m in up if m % 2])
-    expected = (((8.8, 14.7), (18.0, 21.3), (20.0, 24.6)), ((14.0, 20.0), (23.3, 26.6), (25.5, 30.0)), ((9.5, 15.0), (17.5, 21.0), (21.1, 23.0)))
+    expected = (
+        ((8.4, 13.4), (16.4, 19.4), (17.0, 20.8)),
+        ((12.4, 17.4), (20.4, 23.4), (21.0, 25.0)),
+        ((9.5, 15.0), (17.5, 20.0), (20.1, 22.0)),
+        ((16.0, 20.0), (22.7, 25.3), (24.0, 28.0)),
+    )
     when, events = {}, []
     for c in range(len(spans)):
         for kind, (lot, (begin, end)) in enumerate(zip(lots, expected[c])):
@@ -239,17 +245,20 @@
                 time = begin + (end - begin) * n / max(len(lot) - 1, 1)
                 when[c, kind > 0, moved(c, m)] = time
                 events.append((time, len(events), functools.partial(arrive if kind else reduce, c, m)))
-    for region, parts in enumerate(((0, 2), (1,))):
+    for region, parts in enumerate(((0, 2), (1, 3))):
         for first in range(0, ngrid, 2):
-            time = (22.2, 26.8)[region] + (6.0, 2.0)[region] * first / ngrid
+            time = (20.5, 25.5)[region] + (5.0, 2.0)[region] * first / ngrid
             time = max([time] + [when[c, m > 0, m] for c in parts for m in up[first:first + 2]])
             events.append((time, len(events), functools.partial(gradient, region, first)))
 
-    core_t[...] = jnp.transpose(core_ref[...])
-    for p in range(np_all):
-        hi, lo = split(x8[p:p + 1, :] * core_t[...])
-        thi[p // npp, p % npp * vec:(p % npp + 1) * vec, :] = hi
-        tlo[p // npp, p % npp * vec:(p % npp + 1) * vec, :] = lo
+    def turned_factors():
+        core_t[...] = jnp.transpose(core_ref[...])
+        for p in range(np_all):
+            hi, lo = split(x8[p:p + 1, :] * core_t[...])
+            thi[p // npp, p % npp * vec:(p % npp + 1) * vec, :] = hi
+            tlo[p // npp, p % npp * vec:(p % npp + 1) * vec, :] = lo
+
+    events.append((15.5, len(events), turned_factors))
     for _, _, event in sorted(events, key=lambda item: item[:2]):
         event()
 
@@ -400,10 +409,12 @@
     rpad = -(-rows // 16) * 16
     tiles = rpad // 16
     third = max(1, tiles // 6)
-    sizes = [-(-(tiles - third) // 2) * 16, (tiles - third) // 2 * 16, third * 16]
-    chunks = [(0, sizes[0]), (sizes[0] + sizes[2], sizes[1]), (sizes[0], sizes[2])]
+    fourth = (tiles - third) // 4
+    rest = tiles - third - fourth
+    sizes = [(rest - rest // 2) * 16, rest // 2 * 16, third * 16, fourth * 16]
+    chunks = [(0, sizes[0]), (sizes[0] + sizes[2], sizes[1]), (sizes[0], sizes[2]), (rpad - sizes[3], sizes[3])]
     plain = list(range(bits))
-    orders = [plain, plain, plain[1:] + plain[:1]]
+    orders = [plain, plain, plain[1:] + plain[:1], plain]
     cg_scale = -1.0 / math.sqrt(np_all * rows * nrow)
     fg_scale = -math.sqrt(pts * ngrid / (rows * nrow * vec))
     cfg = (nrow, bits, npp, held, rows, rpad, vec, chunks, orders, cg_scale, fg_scale)

time: 57.8 us -> 60.2 us (1.042)
  Pallas kernels: 57 us -> 59.4 us
    pallas_call x1, Pallas kernels: 54.3 us -> 56.6 us  [per_device(): pl.pallas_call(functools.partial(kernel, cfg), out_shape=results, in_spec...]
where the time goes in v6:
time: 60.2 us; the launch traced here: 60 us
  Pallas kernels  59.4 us (99%)
  between operations  0.64 us (1%)
    pallas_call x1, Pallas kernels, per_device(): pl.pallas_call(functools.partial(kernel, cfg), out_shape=results, in_spec...  56.6 us
    pallas_call x1, Pallas kernels, per_device(): pl.pallas_call(hand_out, out_shape=results, in_specs=[pl.BlockSpec(memory...  2.72 us

profile of v6, /device:TPU:0, one launch (start us, length us, event | category | flops | bytes accessed | tf_op | source)
XLA Modules:
  0.0 60.0 jit_solution(8605021750044154704)
XLA Ops:
  0.6 56.6 %hypercontraction.1 = (f32[2400,128]{1,0:T(8,128)}, f32[768,128]{1,0:T(8,128)}, f32[300,768]{1,0:T(8,128)}) custom-call(f32[300,768]{1,0:T(8,128)} %x_hbm.1, f32[768,128]{1,0:T(8,128)} %core_hbm.1, f32[2400,128]{1,0:T(8,128)} %bitcast.10), custom_call_target="tpu_custom_call" | custom-call | flops 4246732800 | bytes 1843200 | tf_op jit(solution)/shard_map/hypercontraction/pallas_call | solution.py:453
  57.3 2.7 %hand_out.1 = (f32[2400,128]{1,0:T(8,128)}, f32[768,128]{1,0:T(8,128)}, f32[300,768]{1,0:T(8,128)}) custom-call(f32[2400,128]{1,0:T(8,128)} %get-tuple-element.9.res_in, f32[768,128]{1,0:T(8,128)} %get-tuple-element.10.cg_in, f32[300,768]{1,0:T(8,128)} %get-tuple-element.11.fg_in), custom_call_target="tpu_custom_call" | custom-call | tf_op jit(solution)/shard_map/hand_out/pallas_call | solution.py:463

commit v7 on v5

--- a/solution.py
+++ b/solution.py
@@ -245,11 +245,14 @@
             time = max([time] + [when[c, m > 0, m] for c in parts for m in up[first:first + 2]])
             events.append((time, len(events), functools.partial(gradient, region, first)))
 
-    core_t[...] = jnp.transpose(core_ref[...])
-    for p in range(np_all):
-        hi, lo = split(x8[p:p + 1, :] * core_t[...])
-        thi[p // npp, p % npp * vec:(p % npp + 1) * vec, :] = hi
-        tlo[p // npp, p % npp * vec:(p % npp + 1) * vec, :] = lo
+    def turned_factors():
+        core_t[...] = jnp.transpose(core_ref[...])
+        for p in range(np_all):
+            hi, lo = split(x8[p:p + 1, :] * core_t[...])
+            thi[p // npp, p % npp * vec:(p % npp + 1) * vec, :] = hi
+            tlo[p // npp, p % npp * vec:(p % npp + 1) * vec, :] = lo
+
+    events.append((16.5, len(events), turned_factors))
     for _, _, event in sorted(events, key=lambda item: item[:2]):
         event()
 
@@ -400,7 +403,8 @@
     rpad = -(-rows // 16) * 16
     tiles = rpad // 16
     third = max(1, tiles // 6)
-    sizes = [-(-(tiles - third) // 2) * 16, (tiles - third) // 2 * 16, third * 16]
+    less = (tiles - third) * 7 // 16
+    sizes = [(tiles - third - less) * 16, less * 16, third * 16]
     chunks = [(0, sizes[0]), (sizes[0] + sizes[2], sizes[1]), (sizes[0], sizes[2])]
     plain = list(range(bits))
     orders = [plain, plain, plain[1:] + plain[:1]]

time: 57.8 us -> 59 us (1.021)
  Pallas kernels: 57 us -> 58.2 us
    pallas_call x1, Pallas kernels: 54.3 us -> 55.5 us  [per_device(): pl.pallas_call(functools.partial(kernel, cfg), out_shape=results, in_spec...]
where the time goes in v7:
time: 59 us; the launch traced here: 58.8 us
  Pallas kernels  58.2 us (99%)
  between operations  0.64 us (1%)
    pallas_call x1, Pallas kernels, per_device(): pl.pallas_call(functools.partial(kernel, cfg), out_shape=results, in_spec...  55.5 us
    pallas_call x1, Pallas kernels, per_device(): pl.pallas_call(hand_out, out_shape=results, in_specs=[pl.BlockSpec(memory...  2.72 us

profile of v7, /device:TPU:0, one launch (start us, length us, event | category | flops | bytes accessed | tf_op | source)
XLA Modules:
  0.0 58.8 jit_solution(15117198724902351946)
XLA Ops:
  0.6 55.5 %hypercontraction.1 = (f32[2400,128]{1,0:T(8,128)}, f32[768,128]{1,0:T(8,128)}, f32[300,768]{1,0:T(8,128)}) custom-call(f32[300,768]{1,0:T(8,128)} %x_hbm.1, f32[768,128]{1,0:T(8,128)} %core_hbm.1, f32[2400,128]{1,0:T(8,128)} %bitcast.10), custom_call_target="tpu_custom_call" | custom-call | flops 4246732800 | bytes 1843200 | tf_op jit(solution)/shard_map/hypercontraction/pallas_call | solution.py:446
  56.1 2.7 %hand_out.1 = (f32[2400,128]{1,0:T(8,128)}, f32[768,128]{1,0:T(8,128)}, f32[300,768]{1,0:T(8,128)}) custom-call(f32[2400,128]{1,0:T(8,128)} %get-tuple-element.9.res_in, f32[768,128]{1,0:T(8,128)} %get-tuple-element.10.cg_in, f32[300,768]{1,0:T(8,128)} %get-tuple-element.11.fg_in), custom_call_target="tpu_custom_call" | custom-call | tf_op jit(solution)/shard_map/hand_out/pallas_call | solution.py:456
